TPU v7x, 256 devices: a whole 4x4x8 slice. The times are simulated.
256 devices in a mesh: row: 8 (over z_hi, core), col: 32 (over x, z_lo, y).
Axes of the slice: x: 4, y: 4, z: 8 (z_hi: 4, z_lo: 2; z = z_hi * 2 + z_lo), core: 2. Of those that a mesh axis runs over, the one named last changes fastest.
Arguments:
- node_feats: bfloat16 [2048, 25, 128], P(('row', 'col')), may hold values from -6 to 6
- grad_out: bfloat16 [2048, 25, 128], P(('row', 'col')), may hold values from -6 to 6
- edge_src: int32 [8, 32, 512], P('row', 'col'), may hold values from 0 to 63
- edge_tgt: int32 [8, 32, 512], P('row', 'col'), may hold values from 0 to 255
- edge_counts: int32 [8, 32], P('row', 'col'), may hold values from 64 to 512, as said below
- wigner: bfloat16 [8, 32, 512, 475], P('row', 'col'), may hold values from -1 to 1, as said below
- w_zero: bfloat16 [1280, 640], replicated, may hold values from -0.15625 to 0.15625
- w_one: bfloat16 [2, 1024, 512], replicated, may hold values from -0.1875 to 0.1875
- w_two: bfloat16 [2, 768, 384], replicated, may hold values from -0.21875 to 0.21875
Outputs:
- grad_nodes: float32 [2048, 25, 128], P(('row', 'col'))
Inputs may be any that keep to these rules, and one draw needn't show every extreme that they name: `edge_counts`: slots at or past a tile's count are ignored. In every row of tiles one tile holds exactly 512 edges. `edge_src`: slot values at or past the tile's count are arbitrary but in range. `edge_tgt`: slot values at or past the tile's count are arbitrary but in range. `wigner`: for every degree l, the rows of orders -2..2 (as far as l allows) hold the matching rows of an orthogonal (2l+1) x (2l+1) block in the columns of degree l, column index l*l + l + m; all other entries are zero.
All inputs are finite; a program needn't handle non-finite values.
Results may differ from a plain program's by a relative error of at most 0.015.
Values may be sent and summed in bfloat16 or wider, within the bound.
A program may use at most 64 MiB of HBM per device.

v0:
```python
import jax
import jax.numpy as jnp
from jax import lax
from jax.sharding import PartitionSpec as P

E_CAP = 512
C = 128
COEF = 25


def so2_apply(edge_in, w_zero, w_one, w_two):
    edge_count = edge_in.shape[0]
    zero_part = jnp.dot(
        edge_in[:, 0:5].reshape(edge_count, -1), w_zero, preferred_element_type=jnp.float32
    )
    outputs = [zero_part.reshape(edge_count, 5, -1)]
    for first_row, row_count, weights in ((5, 4, w_one), (13, 3, w_two)):
        plus_part = edge_in[:, first_row : first_row + row_count].reshape(edge_count, -1)
        minus_part = edge_in[:, first_row + row_count : first_row + 2 * row_count].reshape(
            edge_count, -1
        )
        stacked = jnp.concatenate([plus_part, minus_part], axis=0)
        real_out = jnp.dot(stacked, weights[0], preferred_element_type=jnp.float32)
        imag_out = jnp.dot(stacked, weights[1], preferred_element_type=jnp.float32)
        outputs.append(
            (real_out[:edge_count] - imag_out[edge_count:]).reshape(edge_count, row_count, -1)
        )
        outputs.append(
            (real_out[edge_count:] + imag_out[:edge_count]).reshape(edge_count, row_count, -1)
        )
    return jnp.concatenate(outputs, axis=1)


def so2_transpose(grad_y, w_zero, w_one, w_two):
    edge_count = grad_y.shape[0]
    zero_part = jnp.dot(
        grad_y[:, 0:5].reshape(edge_count, -1), w_zero.T, preferred_element_type=jnp.float32
    )
    outputs = [zero_part.reshape(edge_count, 5, -1)]
    for first_row, row_count, weights in ((5, 4, w_one), (13, 3, w_two)):
        plus_grad = grad_y[:, first_row : first_row + row_count].reshape(edge_count, -1)
        minus_grad = grad_y[:, first_row + row_count : first_row + 2 * row_count].reshape(
            edge_count, -1
        )
        stacked = jnp.concatenate([plus_grad, minus_grad], axis=0)
        real_back = jnp.dot(stacked, weights[0].T, preferred_element_type=jnp.float32)
        imag_back = jnp.dot(stacked, weights[1].T, preferred_element_type=jnp.float32)
        outputs.append(
            (real_back[:edge_count] + imag_back[edge_count:]).reshape(edge_count, row_count, -1)
        )
        outputs.append(
            (real_back[edge_count:] - imag_back[:edge_count]).reshape(edge_count, row_count, -1)
        )
    return jnp.concatenate(outputs, axis=1)


def edge_grads(src_feats, tgt_feats, cotangent, matrix, weights):
    w_zero, w_one, w_two = weights

    def rotate(values):
        return jnp.einsum("ekj,ejc->ekc", matrix, values, preferred_element_type=jnp.float32)

    def unrotate(values):
        return jnp.einsum("ekj,ekc->ejc", matrix, values, preferred_element_type=jnp.float32)

    edge_in = jnp.concatenate([rotate(src_feats), rotate(tgt_feats)], axis=2).astype(jnp.bfloat16)
    rotated_cot = rotate(cotangent).astype(jnp.bfloat16)
    output = so2_apply(edge_in, w_zero, w_one, w_two)
    scalar = output[:, 0]
    gating = jax.nn.sigmoid(scalar)
    gate_slope = gating * (1.0 - gating)
    higher = rotated_cot[:, 1:].astype(jnp.float32)
    gate_grad = jnp.sum(higher * output[:, 1:], axis=1)
    first_cot = rotated_cot[:, 0].astype(jnp.float32)
    scalar_grad = first_cot * (gating + scalar * gate_slope) + gate_grad * gate_slope
    grad_y = jnp.concatenate([scalar_grad[:, None], gating[:, None] * higher], axis=1).astype(
        jnp.bfloat16
    )
    grad_in = so2_transpose(grad_y, w_zero, w_one, w_two).astype(jnp.bfloat16)
    channels = cotangent.shape[2]
    grad_src = unrotate(grad_in[:, :, :channels]).astype(jnp.bfloat16)
    grad_tgt = unrotate(grad_in[:, :, channels:]).astype(jnp.bfloat16)
    return (grad_src, grad_tgt)


def run_edges(
    source_list,
    target_list,
    rotations,
    source_feats,
    target_feats,
    target_cot,
    upper,
    totals,
    weights,
):
    block_size = min(128, E_CAP)
    source_list = jnp.concatenate([source_list, jnp.zeros((block_size,), jnp.int32)])
    target_list = jnp.concatenate([target_list, jnp.zeros((block_size,), jnp.int32)])
    rotations = jnp.concatenate(
        [rotations, jnp.zeros((block_size, rotations.shape[1]), rotations.dtype)]
    )
    target_ids = jnp.arange(target_feats.shape[0], dtype=jnp.int32)
    source_ids = jnp.arange(source_feats.shape[0], dtype=jnp.int32)
    block_count = (upper + block_size - 1) // block_size

    def block_step(block_index, running):
        start_slot = block_index * block_size
        source_rows = lax.dynamic_slice_in_dim(source_list, start_slot, block_size)
        target_rows = lax.dynamic_slice_in_dim(target_list, start_slot, block_size)
        matrix = lax.dynamic_slice_in_dim(rotations, start_slot, block_size, 0).reshape(
            block_size, 19, 25
        )
        in_range = start_slot + jnp.arange(block_size, dtype=jnp.int32) < upper
        grad_src, grad_tgt = edge_grads(
            source_feats[source_rows],
            target_feats[target_rows],
            target_cot[target_rows],
            matrix,
            weights,
        )
        target_hot = ((target_rows[None, :] == target_ids[:, None]) & in_range[None, :]).astype(
            jnp.bfloat16
        )
        source_hot = ((source_rows[None, :] == source_ids[:, None]) & in_range[None, :]).astype(
            jnp.bfloat16
        )
        new_target = running[0] + jnp.dot(
            target_hot, grad_tgt.reshape(block_size, -1), preferred_element_type=jnp.float32
        )
        new_source = running[1] + jnp.dot(
            source_hot, grad_src.reshape(block_size, -1), preferred_element_type=jnp.float32
        )
        return (new_target, new_source)

    return lax.fori_loop(0, block_count, block_step, totals)


def rounded(values):
    narrow = lax.optimization_barrier(values.astype(jnp.bfloat16))
    return narrow.astype(jnp.float32)


def local(node_feats, grad_out, edge_src, edge_tgt, edge_counts, wigner, w_zero, w_one, w_two):
    target_cot, target_feats = (
        lax.all_gather(grad_out, "col", axis=0, tiled=True),
        lax.all_gather(node_feats, "col", axis=0, tiled=True),
    )
    source_feats = lax.all_gather(node_feats, "row", axis=0, tiled=True)
    weights = (w_zero, w_one, w_two)
    own_src = edge_src[0, 0]
    own_tgt = edge_tgt[0, 0]
    own_count = edge_counts[0, 0]
    own_rot = wigner[0, 0]
    empty_target = jnp.zeros((target_feats.shape[0], COEF * C), jnp.float32)
    empty_source = jnp.zeros((source_feats.shape[0], COEF * C), jnp.float32)
    target_sum, source_sum = run_edges(
        own_src,
        own_tgt,
        own_rot,
        source_feats,
        target_feats,
        target_cot,
        own_count,
        (empty_target, empty_source),
        weights,
    )
    own_part = lax.psum_scatter(
        rounded(target_sum).astype(jnp.bfloat16), "col", scatter_dimension=0, tiled=True
    ).astype(jnp.float32)
    cross_part = lax.psum_scatter(
        rounded(source_sum).astype(jnp.bfloat16), "row", scatter_dimension=0, tiled=True
    ).astype(jnp.float32)
    return (own_part + cross_part).reshape(own_part.shape[0], COEF, C)


def solution(mesh):
    placed = (
        P(("row", "col"), None, None),
        P(("row", "col"), None, None),
        P("row", "col", None),
        P("row", "col", None),
        P("row", "col"),
        P("row", "col", None, None),
        P(),
        P(),
        P(),
    )
    return jax.shard_map(
        local, mesh=mesh, in_specs=placed, out_specs=P(("row", "col"), None, None), check_vma=False
    )
```

profile of v0, /device:TPU:2, one launch (start us, length us, event | category | flops | bytes accessed | tf_op | source)
XLA Modules:
  0.0 900.5 jit_solution(12202935970099814985)
XLA Ops:
  10.1 20.0 %all_gather.10 = bf16[64,25,128]{2,0,1:T(8,128)(2,1)S(1)} all-gather(bf16[8,25,128]{2,0,1:T(8,128)(2,1)} %param.11), channel_id=1, replica_groups=mesh['row'=8,'col'=32] {'row'}, dimensions={0}, use_global_device_ids=true | all-gather | bytes 460800 | tf_op jit(solution)/shard_map/all_gather | solution.py:149
  31.1 2.7 copy.206
  34.8 101.3 %all-gather.5.cloned.1.call-done = bf16[256,25,128]{2,0,1:T(8,128)(2,1)} async-done(((bf16[8,25,128]{2,0,1:T(8,128)(2,1)}), bf16[256,25,128]{2,0,1:T(8,128)(2,1)}) %all-gather.5.cloned.1.call-update) | async-done | bytes 1638416 | tf_op jit(solution)/shard_map/all_gather | solution.py:147
  136.1 3.9 copy.205
  140.0 123.0 %all-gather.3.cloned.1.call-done = bf16[256,25,128]{2,0,1:T(8,128)(2,1)} async-done(((bf16[8,25,128]{2,0,1:T(8,128)(2,1)}), bf16[256,25,128]{2,0,1:T(8,128)(2,1)}) %all-gather.3.cloned.1.call-update) | async-done | bytes 1638416 | tf_op jit(solution)/shard_map/all_gather | solution.py:146
  263.0 3.9 copy.203
  269.7 184.5 %while.13 = (s32[]{:T(128)}, f32[256,3200]{1,0:T(8,128)}, f32[64,3200]{1,0:T(8,128)}, s32[]{:T(128)}, s32[640]{0:T(1024)S(1)}, /*index=5*/s32[]{:T(128)}, bf16[6...) while((s32[]{:T(128)}, f32[256,3200]{1,0:T(8,128)}, ...), condition=%wide.region_2.3_spmd.clone, body=%wide.region_0.2_spmd.clone.sunk | while | flops 2448665600 | bytes 127104752 | solution.py:136
  274.3 2.4 gather_fusion.2
  278.2 2.3 gather_fusion.1
  316.0 2.9 copy.271
  324.4 2.5 convolution_add_fusion.5
  326.9 4.3 convolution_add_fusion.4
  335.8 2.4 gather_fusion.2
  339.7 2.3 gather_fusion.1
  377.6 2.9 copy.271
  385.9 2.5 convolution_add_fusion.5
  388.4 4.3 convolution_add_fusion.4
  397.3 2.4 gather_fusion.2
  439.1 2.9 copy.271
  447.4 2.5 convolution_add_fusion.5
  449.9 4.3 convolution_add_fusion.4
  456.3 3.3 convert_element_type.37
  462.6 126.8 %all-reduce.10.cloned.1.call-done = bf16[64,3200]{1,0:T(8,128)(2,1)} async-done(((bf16[64,3200]{1,0:T(8,128)(2,1)}), bf16[64,3200]{1,0:T(8,128)(2,1)}) %all-reduce.10.cloned.1.call-update) | async-done | bytes 409616
  589.4 303.1 %all-reduce.8.cloned.1.call-done = bf16[256,3200]{1,0:T(8,128)(2,1)} async-done(((bf16[256,3200]{1,0:T(8,128)(2,1)}), bf16[256,3200]{1,0:T(8,128)(2,1)}) %all-reduce.8.cloned.1.call-update) | async-done | bytes 1638416
  (337 shorter events, 155.1 us)
Async XLA Ops:
  6.5 129.6 %all-gather.5.cloned.1.call-start = ((), (), s32[]{:S(2)}) async-start(), calls=%async_computation.1 | async-start | bytes 1689600 | tf_op jit(solution)/shard_map/all_gather | solution.py:147
  7.3 255.8 %all-gather.3.cloned.1.call-start = ((), (), s32[]{:S(2)}) async-start(), calls=%async_computation | async-start | bytes 1689600 | tf_op jit(solution)/shard_map/all_gather | solution.py:146
  8.0 581.4 %all-reduce.10.cloned.1.call-start = ((), (), s32[]{:S(2)}) async-start(), calls=%async_computation.3 | async-start | bytes 819200
  31.1 2.8 copy-start.12
  269.7 4.0 copy-start.13
  290.6 6.3 copy-start.5
  296.9 2.3 copy-start.10
  316.0 2.9 copy-start.11
  326.9 4.3 copy-start.1
  326.9 4.3 copy-start.14
  331.2 4.0 copy-start.13
  352.1 6.3 copy-start.5
  358.4 2.2 copy-start.9
  358.4 2.3 copy-start.10
  377.6 2.9 copy-start.11
  388.4 4.3 copy-start.1
  388.4 4.3 copy-start.14
  392.7 4.0 copy-start.13
  413.6 6.3 copy-start.5
  419.9 2.3 copy-start.10
  439.1 2.9 copy-start.11
  449.9 4.3 copy-start.1
  449.9 4.3 copy-start.14
  456.2 436.3 %all-reduce.8.cloned.1.call-start = ((), (), s32[]{:S(2)}) async-start(), calls=%async_computation.2 | async-start | bytes 3276800
  (25 other events, 41.4 us)
Sparse Core Ops, SparseCore 0:
  9.1 127.0 all-gather.4
  137.8 125.1 all-gather.2
  456.3 133.0 all-reduce.9
  592.1 300.3 all-reduce.7
where the time goes:
time: 912 us; the launch traced here: 901 us
  waiting for transfers between devices  656 us (72%)
  local copies, waits for them, and re-layouts  130 us (14%)
  matrix products  58.6 us (6%)
  blocking collectives  20 us (2%)
  other arithmetic  19.3 us (2%)
  between operations  15 us (2%)
    unnamed x6, waiting for transfers between devices  431 us
    all_gather x1, waiting for transfers between devices, local(): lax.all_gather(grad_out, 'col', axis=0, tiled=True)  123 us
    all_gather x1, waiting for transfers between devices, local(): lax.all_gather(node_feats, 'col', axis=0, tiled=True)  101 us
    all_gather x1, blocking collectives, local(): source_feats = lax.all_gather(node_feats, 'row', axis=0, tiled=True)  20 us
  transfers between devices with their start and end apart: 4, of which 4 were waited for; matrix products, arithmetic and copies ran while one was open for 2% of the time, Pallas kernels for 0%

commit v1 on v0

v1 whole, which is shorter than its diff:
```python
import jax
import jax.numpy as jnp
from jax import lax
from jax.experimental import pallas as pl
from jax.experimental.pallas import tpu as pltpu
from jax.sharding import PartitionSpec as P

MESH = pl.DeviceIdType.MESH
F32 = jnp.float32
BF16 = jnp.bfloat16

ROWS = 8
COLS = 32
A = 8
E = 512
C = 128
COEF = 25
PAIRS = 13
FRAME = 19
GROUP = 16
BLOCK = 256
TGT = COLS * A
SRC = ROWS * A
VMEM_LIMIT = 58 * 1024 * 1024


def frame_rows(degree):
    rows = [degree]
    if degree >= 1:
        rows += [5 + degree - 1, 9 + degree - 1]
    if degree >= 2:
        rows += [13 + degree - 2, 16 + degree - 2]
    return rows


def degree_cols(degree):
    return list(range(degree * degree, (degree + 1) * (degree + 1)))


def greet():
    row = lax.axis_index("row")
    col = lax.axis_index("col")
    barrier = pltpu.get_barrier_semaphore()
    for step in range(1, COLS):
        pl.semaphore_signal(
            barrier, inc=1, device_id={"col": lax.rem(col + step, COLS)}, device_id_type=MESH
        )
    for step in range(1, ROWS):
        pl.semaphore_signal(
            barrier, inc=1, device_id={"row": lax.rem(row + step, ROWS)}, device_id_type=MESH
        )
    pl.semaphore_wait(barrier, COLS - 1 + ROWS - 1)
    return row, col


def gather_kernel(feats, cots, g_out, s_out, packed, col_send, col_recv, row_send, row_recv, own):
    packed[:, :, 0:C] = feats[...]
    packed[:, :, C : 2 * C] = cots[...]
    row, col = greet()
    copies = []
    for step in range(1, COLS):
        copies.append(
            pltpu.make_async_remote_copy(
                src_ref=packed,
                dst_ref=g_out.at[col],
                send_sem=col_send.at[step],
                recv_sem=col_recv.at[step],
                device_id={"col": lax.rem(col + step, COLS)},
                device_id_type=MESH,
            )
        )
        copies[-1].start()
    for step in range(1, ROWS):
        copies.append(
            pltpu.make_async_remote_copy(
                src_ref=feats,
                dst_ref=s_out.at[row],
                send_sem=row_send.at[step],
                recv_sem=row_recv.at[step],
                device_id={"row": lax.rem(row + step, ROWS)},
                device_id_type=MESH,
            )
        )
        copies[-1].start()
    mine = pltpu.make_async_copy(packed, g_out.at[col], own.at[0])
    also = pltpu.make_async_copy(feats, s_out.at[row], own.at[1])
    mine.start()
    also.start()
    mine.wait()
    also.wait()
    for copy in copies:
        copy.wait()


def gather(feats, cots):
    return pl.pallas_call(
        gather_kernel,
        out_shape=(
            jax.ShapeDtypeStruct((COLS, COEF, A, 2 * C), BF16),
            jax.ShapeDtypeStruct((ROWS, COEF, A, C), BF16),
        ),
        in_specs=[pl.BlockSpec(memory_space=pltpu.VMEM)] * 2,
        out_specs=(pl.BlockSpec(memory_space=pl.ANY),) * 2,
        scratch_shapes=[
            pltpu.VMEM((COEF, A, 2 * C), BF16),
            pltpu.SemaphoreType.DMA((COLS,)),
            pltpu.SemaphoreType.DMA((COLS,)),
            pltpu.SemaphoreType.DMA((ROWS,)),
            pltpu.SemaphoreType.DMA((ROWS,)),
            pltpu.SemaphoreType.DMA((2,)),
        ],
        compiler_params=pltpu.CompilerParams(
            collective_id=0, has_side_effects=True, vmem_limit_bytes=VMEM_LIMIT
        ),
        name="gather_blocks",
    )(feats, cots)


def reduce_kernel(tgt, src, out, tgt_in, src_in, col_send, col_recv, row_send, row_recv, own):
    row, col = greet()
    copies = []
    for step in range(1, COLS):
        there = lax.rem(col + step, COLS)
        copies.append(
            pltpu.make_async_remote_copy(
                src_ref=tgt.at[there],
                dst_ref=tgt_in.at[col],
                send_sem=col_send.at[step],
                recv_sem=col_recv.at[step],
                device_id={"col": there},
                device_id_type=MESH,
            )
        )
        copies[-1].start()
    for step in range(1, ROWS):
        there = lax.rem(row + step, ROWS)
        copies.append(
            pltpu.make_async_remote_copy(
                src_ref=src.at[there],
                dst_ref=src_in.at[row],
                send_sem=row_send.at[step],
                recv_sem=row_recv.at[step],
                device_id={"row": there},
                device_id_type=MESH,
            )
        )
        copies[-1].start()
    mine = pltpu.make_async_copy(tgt.at[col], tgt_in.at[col], own.at[0])
    also = pltpu.make_async_copy(src.at[row], src_in.at[row], own.at[1])
    mine.start()
    also.start()
    mine.wait()
    also.wait()
    for copy in copies:
        copy.wait()

    def add(j, carry):
        total = jnp.sum(tgt_in[:, j].astype(F32), axis=0)
        out[j] = total + jnp.sum(src_in[:, j].astype(F32), axis=0)
        return carry

    lax.fori_loop(0, COEF, add, 0)


def reduce(tgt, src):
    return pl.pallas_call(
        reduce_kernel,
        out_shape=jax.ShapeDtypeStruct((COEF, A, C), F32),
        in_specs=[pl.BlockSpec(memory_space=pl.ANY)] * 2,
        out_specs=pl.BlockSpec(memory_space=pltpu.VMEM),
        scratch_shapes=[
            pltpu.VMEM((COLS, COEF, A, C), BF16),
            pltpu.VMEM((ROWS, COEF, A, C), BF16),
            pltpu.SemaphoreType.DMA((COLS,)),
            pltpu.SemaphoreType.DMA((COLS,)),
            pltpu.SemaphoreType.DMA((ROWS,)),
            pltpu.SemaphoreType.DMA((ROWS,)),
            pltpu.SemaphoreType.DMA((2,)),
        ],
        compiler_params=pltpu.CompilerParams(
            collective_id=1, has_side_effects=True, vmem_limit_bytes=VMEM_LIMIT
        ),
        name="reduce_blocks",
    )(tgt, src)


def dot(x, y):
    return jnp.dot(x, y, preferred_element_type=F32)


def dot_t(x, y):
    return lax.dot_general(x, y, (((1,), (1,)), ((), ())), preferred_element_type=F32)


def edge_kernel(
    count, src_ids, tgt_ids, rot, g, s, w0, w1, w2, tgt_out, src_out,
    full1, full2, hot_t, hot_s, back_t, back_s, xt, xs, frame, cot, y,
):
    for weights, full in ((w1, full1), (w2, full2)):
        k, n = weights.shape[1:]
        full[0:k, 0:n] = weights[0]
        full[0:k, n : 2 * n] = weights[1]
        full[k : 2 * k, 0:n] = -weights[1]
        full[k : 2 * k, n : 2 * n] = weights[0]

    tgt_row = tgt_ids[...]
    src_row = src_ids[...]
    valid = lax.broadcasted_iota(jnp.int32, (1, E), 1) < count[0, 0]
    marked_t = jnp.where(valid, tgt_row, -1)
    marked_s = jnp.where(valid, src_row, -1)
    back_t[...] = (marked_t == lax.broadcasted_iota(jnp.int32, (TGT, E), 0)).astype(F32).astype(BF16)
    back_s[...] = (marked_s == lax.broadcasted_iota(jnp.int32, (SRC, E), 0)).astype(F32).astype(BF16)
    tgt_col = jnp.transpose(jnp.broadcast_to(tgt_row, (C, E)))
    src_col = jnp.transpose(jnp.broadcast_to(src_row, (C, E)))
    lane = lax.broadcasted_iota(jnp.int32, (E, C), 1)
    hot_t[:, 0:C] = (tgt_col == lane).astype(F32).astype(BF16)
    hot_t[:, C : 2 * C] = (tgt_col == lane + C).astype(F32).astype(BF16)
    hot_s[...] = (src_col == lane)[:, 0:SRC].astype(F32).astype(BF16)

    def gather_tgt(j, carry):
        block = g[:, j].astype(F32).reshape(TGT, 2 * C).astype(BF16)
        xt[j] = dot(hot_t[...], block).astype(BF16)
        return carry

    lax.fori_loop(0, COEF, gather_tgt, 0)

    def gather_src(p, carry):
        first = s[:, 2 * p].astype(F32).reshape(SRC, C)
        second = s[:, jnp.minimum(2 * p + 1, COEF - 1)].astype(F32).reshape(SRC, C)
        block = jnp.concatenate([first, second], axis=1).astype(BF16)
        xs[p] = dot(hot_s[...], block).astype(BF16)
        return carry

    lax.fori_loop(0, PAIRS, gather_src, 0)

    def half(j):
        return slice((j % 2) * C, (j % 2) * C + C)

    def rotate(i, carry):
        at = pl.ds(pl.multiple_of(i * GROUP, GROUP), GROUP)
        matrix = rot[at, :].astype(F32)
        for degree in range(5):
            cols = degree_cols(degree)
            from_src = [xs[j // 2, at, half(j)].astype(F32) for j in cols]
            from_tgt = [xt[j, at, 0:C].astype(F32) for j in cols]
            from_cot = [xt[j, at, C : 2 * C].astype(F32) for j in cols]
            for k in frame_rows(degree):
                sums = [None, None, None]
                for n, j in enumerate(cols):
                    entry = k * COEF + j
                    factor = jnp.broadcast_to(matrix[:, entry : entry + 1], (GROUP, C))
                    for which, values in enumerate((from_src, from_tgt, from_cot)):
                        term = factor * values[n]
                        sums[which] = term if sums[which] is None else sums[which] + term
                frame[at, 2 * k * C : (2 * k + 1) * C] = sums[0].astype(BF16)
                frame[at, (2 * k + 1) * C : (2 * k + 2) * C] = sums[1].astype(BF16)
                cot[at, k * C : (k + 1) * C] = sums[2].astype(BF16)
        return carry

    lax.fori_loop(0, E // GROUP, rotate, 0)

    parts = ((0, 5, w0), (5, 8, full1), (13, 6, full2))

    def forward(i, carry):
        at = pl.ds(pl.multiple_of(i * BLOCK, BLOCK), BLOCK)
        for first, rows, weights in parts:
            y[at, first * C : (first + rows) * C] = dot(
                frame[at, 2 * first * C : 2 * (first + rows) * C], weights[...]
            )
        return carry

    lax.fori_loop(0, E // BLOCK, forward, 0)

    def gate(i, carry):
        at = pl.ds(pl.multiple_of(i * GROUP, GROUP), GROUP)
        scalar = y[at, 0:C]
        gating = jax.nn.sigmoid(scalar)
        slope = gating * (1.0 - gating)
        total = jnp.zeros((GROUP, C), F32)
        for k in range(1, FRAME):
            piece = slice(k * C, (k + 1) * C)
            value = cot[at, piece].astype(F32)
            total = total + value * y[at, piece]
            cot[at, piece] = (gating * value).astype(BF16)
        first = cot[at, 0:C].astype(F32)
        cot[at, 0:C] = (first * (gating + scalar * slope) + total * slope).astype(BF16)
        return carry

    lax.fori_loop(0, E // GROUP, gate, 0)

    def backward(i, carry):
        at = pl.ds(pl.multiple_of(i * BLOCK, BLOCK), BLOCK)
        for first, rows, weights in parts:
            frame[at, 2 * first * C : 2 * (first + rows) * C] = dot_t(
                cot[at, first * C : (first + rows) * C], weights[...]
            ).astype(BF16)
        return carry

    lax.fori_loop(0, E // BLOCK, backward, 0)

    def unrotate(i, carry):
        at = pl.ds(pl.multiple_of(i * GROUP, GROUP), GROUP)
        matrix = rot[at, :].astype(F32)
        for degree in range(5):
            rows = frame_rows(degree)
            of_src = [frame[at, 2 * k * C : (2 * k + 1) * C].astype(F32) for k in rows]
            of_tgt = [frame[at, (2 * k + 1) * C : (2 * k + 2) * C].astype(F32) for k in rows]
            for j in degree_cols(degree):
                sums = [None, None]
                for n, k in enumerate(rows):
                    entry = k * COEF + j
                    factor = jnp.broadcast_to(matrix[:, entry : entry + 1], (GROUP, C))
                    for which, values in enumerate((of_src, of_tgt)):
                        term = factor * values[n]
                        sums[which] = term if sums[which] is None else sums[which] + term
                xs[j // 2, at, half(j)] = sums[0].astype(BF16)
                xt[j // 2, at, half(j)] = sums[1].astype(BF16)
        return carry

    lax.fori_loop(0, E // GROUP, unrotate, 0)

    for p in range(PAIRS):
        for back, grads, out, blocks in ((back_t, xt, tgt_out, COLS), (back_s, xs, src_out, ROWS)):
            both = dot(back[...], grads[p])
            for j in (2 * p, 2 * p + 1):
                if j < COEF:
                    out[:, j] = both[:, half(j)].reshape(blocks, A, C).astype(BF16)


def edges(count, src_ids, tgt_ids, rot, g, s, w0, w1, w2):
    vmem = pl.BlockSpec(memory_space=pltpu.VMEM)
    return pl.pallas_call(
        edge_kernel,
        out_shape=(
            jax.ShapeDtypeStruct((COLS, COEF, A, C), BF16),
            jax.ShapeDtypeStruct((ROWS, COEF, A, C), BF16),
        ),
        in_specs=[pl.BlockSpec(memory_space=pltpu.SMEM)] + [vmem] * 8,
        out_specs=(vmem, vmem),
        scratch_shapes=[
            pltpu.VMEM((2 * w1.shape[1], 2 * w1.shape[2]), BF16),
            pltpu.VMEM((2 * w2.shape[1], 2 * w2.shape[2]), BF16),
            pltpu.VMEM((E, TGT), BF16),
            pltpu.VMEM((E, SRC), BF16),
            pltpu.VMEM((TGT, E), BF16),
            pltpu.VMEM((SRC, E), BF16),
            pltpu.VMEM((COEF, E, 2 * C), BF16),
            pltpu.VMEM((PAIRS, E, 2 * C), BF16),
            pltpu.VMEM((E, FRAME * 2 * C), BF16),
            pltpu.VMEM((E, FRAME * C), BF16),
            pltpu.VMEM((E, FRAME * C), F32),
        ],
        compiler_params=pltpu.CompilerParams(vmem_limit_bytes=VMEM_LIMIT),
        cost_estimate=pl.CostEstimate(
            flops=12 * 10**9, bytes_accessed=12 * 10**6, transcendentals=E * C
        ),
        name="edge_gradients",
    )(count, src_ids, tgt_ids, rot, g, s, w0, w1, w2)


def local(node_feats, grad_out, edge_src, edge_tgt, edge_counts, wigner, w_zero, w_one, w_two):
    feats = jnp.transpose(node_feats, (1, 0, 2))
    cots = jnp.transpose(grad_out, (1, 0, 2))
    g, s = gather(feats, cots)
    tgt, src = edges(
        edge_counts, edge_src[0], edge_tgt[0], wigner[0, 0], g, s, w_zero, w_one, w_two
    )
    return jnp.transpose(reduce(tgt, src), (1, 0, 2))


def solution(mesh):
    placed = (
        P(("row", "col"), None, None),
        P(("row", "col"), None, None),
        P("row", "col", None),
        P("row", "col", None),
        P("row", "col"),
        P("row", "col", None, None),
        P(),
        P(),
        P(),
    )
    return jax.shard_map(
        local, mesh=mesh, in_specs=placed, out_specs=P(("row", "col"), None, None), check_vma=False
    )
```

time: 912 us -> 171 us (0.19)
  waiting for transfers between devices: 656 us -> 0 us
  Pallas kernels: 0 us -> 164 us
  local copies, waits for them, and re-layouts: 130 us -> 3.58 us
  matrix products: 58.6 us -> 0 us
  blocking collectives: 20 us -> 0 us
  other arithmetic: 19.3 us -> 0 us
  between operations: 15 us -> 0.67 us
    unnamed x6 -> x0, waiting for transfers between devices: 431 us -> none
    all_gather x2 -> x0, waiting for transfers between devices: 224 us -> none  [the longest x1 123 us: local(): lax.all_gather(grad_out, 'col', axis=0, tiled=True)]
    pallas_call x0 -> x3, Pallas kernels: none -> 164 us  [the longest x1 77.9 us: gather(): pl.pallas_call(gather_kernel, out_shape=(jax.ShapeDtypeStruct((COLS, COEF...]
    dot_general x51 -> x0, matrix products: 58.6 us -> none  [the longest x3 13 us: block_step(): jnp.dot(target_hot, grad_tgt.reshape(block_size, -1), preferred_element_t...]
    slice x33 -> x0, local copies, waits for them, and re-layouts: 26.7 us -> none  [the longest x12 10.4 us: so2_transpose(): grad_y[:, first_row:first_row + row_count].reshape(edge_count, -1)]
    all_gather x1 -> x0, blocking collectives: 20 us -> none  [local(): source_feats = lax.all_gather(node_feats, 'row', axis=0, tiled=True)]
    reshape x30 -> x0, local copies, waits for them, and re-layouts: 19.6 us -> none  [the longest x6 7.84 us: so2_apply(): (real_out[edge_count:] + imag_out[:edge_count]).reshape(edge_count, row_c...]
    gather x9 -> x0, local copies, waits for them, and re-layouts: 19.5 us -> none  [the longest x3 7.05 us: block_step(): target_cot[target_rows]]
  transfers between devices with their start and end apart: 4 -> 0, of which waited for: 4 -> 0; matrix products, arithmetic and copies ran while one was open for 2% -> 0% of each run, Pallas kernels for 0% -> 0%
where the time goes in v1:
time: 171 us; the launch traced here: 168 us
  Pallas kernels  164 us (96%)
  local copies, waits for them, and re-layouts  3.58 us (2%)
    pallas_call x1, Pallas kernels, gather(): pl.pallas_call(gather_kernel, out_shape=(jax.ShapeDtypeStruct((COLS, COEF...  77.9 us
    pallas_call x1, Pallas kernels, edges(): pl.pallas_call(edge_kernel, out_shape=(jax.ShapeDtypeStruct((COLS, COEF,...  45.7 us
    pallas_call x1, Pallas kernels, reduce(): pl.pallas_call(reduce_kernel, out_shape=jax.ShapeDtypeStruct((COEF, A, C)...  40.2 us
    unnamed x2, local copies, waits for them, and re-layouts  3.58 us

profile of v1, /device:TPU:2, one launch (start us, length us, event | category | flops | bytes accessed | tf_op | source)
XLA Modules:
  0.0 168.1 jit_solution(9886266145440787824)
XLA Ops:
  0.7 2.0 %copy.10 = bf16[1,1,512,475]{3,2,1,0:T(8,128)(2,1)} copy(bf16[1,1,512,475]{2,3,1,0:T(8,128)(2,1)} %param.14) | data formatting | bytes 972800 | tf_op args[5]
  2.7 77.9 %gather_blocks.1 = (bf16[32,25,8,256]{3,2,1,0:T(8,128)(2,1)}, bf16[8,25,8,128]{3,2,1,0:T(8,128)(2,1)}) custom-call(bf16[25,8,128]{2,1,0:T(8,128)(2,1)} %bitcast.8, bf16[25,8,128]{2,1,0:T(8,128)(2,1)} %bitcast.9), custom_call_target="tpu_custom_call" | custom-call | tf_op jit(solution)/shard_map/gather_blocks/pallas_call | solution.py:96
  80.6 45.7 %edge_gradients.1 = (bf16[32,25,8,128]{3,2,1,0:T(8,128)(2,1)}, bf16[8,25,8,128]{3,2,1,0:T(8,128)(2,1)}) custom-call(s32[1,1]{1,0:T(1,128)S(6)} %copy.12.count, s32[1,512]{1,0:T(1,128)} %bitcast.10, s32[1,512]{1,0:T(1,128)} %bitcast.11, bf16[512,475]{1,0:T(8,128)(2,1)} %bitcast.6, bf16[32,25,8,256]{3,2,1,0:T(8,128)(2,1)} %get-tuple-element.9.g, ...), custom_call_target="tpu_custom_call" | custom-call | flops 12000000000 | bytes 12000000 | tf_op jit(solution)/shard_map/edge_gradients/pallas_call | solution.py:332
  126.3 40.2 %reduce_blocks.1 = f32[25,8,128]{2,1,0:T(8,128)} custom-call(bf16[32,25,8,128]{3,2,1,0:T(8,128)(2,1)} %get-tuple-element.11.tgt, bf16[8,25,8,128]{3,2,1,0:T(8,128)(2,1)} %get-tuple-element.12.src), custom_call_target="tpu_custom_call" | custom-call | tf_op jit(solution)/shard_map/reduce_blocks/pallas_call | solution.py:166
  166.5 1.5 copy.13

commit v2 on v1

--- a/solution.py
+++ b/solution.py
@@ -37,76 +37,172 @@
     return list(range(degree * degree, (degree + 1) * (degree + 1)))
 
 
-def greet():
-    row = lax.axis_index("row")
-    col = lax.axis_index("col")
-    barrier = pltpu.get_barrier_semaphore()
-    for step in range(1, COLS):
-        pl.semaphore_signal(
-            barrier, inc=1, device_id={"col": lax.rem(col + step, COLS)}, device_id_type=MESH
+def ring(value, step):
+    return lax.rem(value + step, 4)
+
+
+class Net:
+    def __init__(self, send, recv):
+        row = lax.axis_index("row")
+        col = lax.axis_index("col")
+        self.x = lax.div(col, 8)
+        self.z = lax.rem(lax.div(col, 4), 2)
+        self.y = lax.rem(col, 4)
+        self.high = lax.div(row, 2)
+        self.core = lax.rem(row, 2)
+        self.send = send
+        self.recv = recv
+        self.copies = []
+
+    def at(self, x=0, z=0, y=0):
+        z_now = 1 - self.z if z else self.z
+        return {"col": ring(self.x, x) * 8 + z_now * 4 + ring(self.y, y)}
+
+    def peer(self, high=0, core=0):
+        core_now = 1 - self.core if core else self.core
+        return {"row": ring(self.high, high) * 2 + core_now}
+
+    def greet(self):
+        barrier = pltpu.get_barrier_semaphore()
+        devices = [self.at(x=1), self.at(x=3), self.at(y=1), self.at(y=3), self.at(z=1)]
+        devices += [self.peer(high=step) for step in (1, 2, 3)] + [self.peer(core=1)]
+        for device in devices:
+            pl.semaphore_signal(barrier, inc=1, device_id=device, device_id_type=MESH)
+        pl.semaphore_wait(barrier, len(devices))
+
+    def push(self, source, target, device):
+        n = len(self.copies)
+        copy = pltpu.make_async_remote_copy(
+            src_ref=source,
+            dst_ref=target,
+            send_sem=self.send.at[n],
+            recv_sem=self.recv.at[n],
+            device_id=device,
+            device_id_type=MESH,
         )
-    for step in range(1, ROWS):
-        pl.semaphore_signal(
-            barrier, inc=1, device_id={"row": lax.rem(row + step, ROWS)}, device_id_type=MESH
-        )
-    pl.semaphore_wait(barrier, COLS - 1 + ROWS - 1)
-    return row, col
-
-
-def gather_kernel(feats, cots, g_out, s_out, packed, col_send, col_recv, row_send, row_recv, own):
+        copy.start()
+        self.copies.append(copy)
+        return copy
+
+
+QUARTERS = ((0, 7), (7, 13), (13, 19), (19, 25))
+HALVES = ((0, 13), (13, 25))
+MESSAGES = 96
+
+
+def span(bounds):
+    return pl.ds(bounds[0], bounds[1] - bounds[0])
+
+
+def gather_kernel(feats, cots, g, s, packed, send, recv, own):
     packed[:, :, 0:C] = feats[...]
     packed[:, :, C : 2 * C] = cots[...]
-    row, col = greet()
-    copies = []
-    for step in range(1, COLS):
-        copies.append(
-            pltpu.make_async_remote_copy(
-                src_ref=packed,
-                dst_ref=g_out.at[col],
-                send_sem=col_send.at[step],
-                recv_sem=col_recv.at[step],
-                device_id={"col": lax.rem(col + step, COLS)},
-                device_id_type=MESH,
+    net = Net(send, recv)
+    net.greet()
+    received = []
+
+    def arrived(copy):
+        copy.wait_recv()
+        received.append(copy)
+
+    def place(h, first, second, z, bounds):
+        near, far = (second, first) if h == 0 else (first, second)
+        z_now = 1 - net.z if z else net.z
+        return g.at[ring(net.x, far), z_now, ring(net.y, near), span(bounds)]
+
+    def step_to(h, phase, sign):
+        along_y = (h == 0) == (phase == 0)
+        return net.at(y=sign) if along_y else net.at(x=sign)
+
+    def own_piece(bounds):
+        return packed.at[span(bounds)]
+
+    across = net.push(packed, g.at[net.x, net.z, net.y], net.at(z=1))
+    inner = {}
+    outer = {}
+    for h in (0, 1):
+        for sign in (1, 3):
+            inner[h, 0, sign] = net.push(
+                own_piece(HALVES[h]), place(h, 0, 0, 0, HALVES[h]), step_to(h, 0, sign)
             )
-        )
-        copies[-1].start()
-    for step in range(1, ROWS):
-        copies.append(
-            pltpu.make_async_remote_copy(
-                src_ref=feats,
-                dst_ref=s_out.at[row],
-                send_sem=row_send.at[step],
-                recv_sem=row_recv.at[step],
-                device_id={"row": lax.rem(row + step, ROWS)},
-                device_id_type=MESH,
+    sibling = [net.push(feats, s.at[net.high, net.core], net.peer(core=1))]
+    rows = [net.push(feats, s.at[net.high, net.core], net.peer(high=step)) for step in (1, 3, 2)]
+    for h in (0, 1):
+        for sign in (1, 3):
+            outer[h, 0, 0, sign] = net.push(
+                own_piece(HALVES[h]), place(h, 0, 0, 0, HALVES[h]), step_to(h, 1, sign)
             )
-        )
-        copies[-1].start()
-    mine = pltpu.make_async_copy(packed, g_out.at[col], own.at[0])
-    also = pltpu.make_async_copy(feats, s_out.at[row], own.at[1])
+    mine = pltpu.make_async_copy(packed, g.at[net.x, net.z, net.y], own.at[0])
+    also = pltpu.make_async_copy(feats, s.at[net.high, net.core], own.at[1])
     mine.start()
     also.start()
+
+    def spread(h, near, z):
+        block = place(h, 0, near, z, HALVES[h])
+        for sign in (1, 3):
+            outer[h, z, near, sign] = net.push(block, block, step_to(h, 1, sign))
+
+    arrived(across)
+    for h in (0, 1):
+        block = place(h, 0, 0, 1, HALVES[h])
+        for sign in (1, 3):
+            inner[h, 1, sign] = net.push(block, block, step_to(h, 0, sign))
+    for h in (0, 1):
+        spread(h, 0, 1)
+    passed = {}
+    for z in (0, 1):
+        for sign, quarter in ((1, 0), (3, 1)):
+            for h in (0, 1):
+                arrived(inner[h, z, sign])
+                bounds = QUARTERS[2 * h + quarter]
+                block = place(h, 0, 4 - sign, z, bounds)
+                passed[h, z, sign] = net.push(block, block, step_to(h, 0, sign))
+                spread(h, 4 - sign, z)
+    last = []
+
+    def relay(h, z, near):
+        for sign, quarter in ((1, 0), (3, 1)):
+            arrived(outer[h, z, near, sign])
+            block = place(h, 4 - sign, near, z, QUARTERS[2 * h + quarter])
+            last.append(net.push(block, block, step_to(h, 1, sign)))
+
+    for z in (0, 1):
+        for h in (0, 1):
+            relay(h, z, 0)
+    for z in (0, 1):
+        for h in (0, 1):
+            arrived(passed[h, z, 1])
+            arrived(passed[h, z, 3])
+            spread(h, 2, z)
+    for step, copy in zip((1, 3, 2), rows):
+        arrived(copy)
+        block = s.at[ring(net.high, 4 - step), net.core]
+        sibling.append(net.push(block, block, net.peer(core=1)))
+    for near in (3, 1, 2):
+        for z in (0, 1):
+            for h in (0, 1):
+                relay(h, z, near)
+    for copy in last + sibling:
+        arrived(copy)
     mine.wait()
     also.wait()
-    for copy in copies:
-        copy.wait()
+    for copy in net.copies:
+        copy.wait_send()
 
 
 def gather(feats, cots):
     return pl.pallas_call(
         gather_kernel,
         out_shape=(
-            jax.ShapeDtypeStruct((COLS, COEF, A, 2 * C), BF16),
-            jax.ShapeDtypeStruct((ROWS, COEF, A, C), BF16),
+            jax.ShapeDtypeStruct((4, 2, 4, COEF, A, 2 * C), BF16),
+            jax.ShapeDtypeStruct((4, 2, COEF, A, C), BF16),
         ),
         in_specs=[pl.BlockSpec(memory_space=pltpu.VMEM)] * 2,
         out_specs=(pl.BlockSpec(memory_space=pl.ANY),) * 2,
         scratch_shapes=[
             pltpu.VMEM((COEF, A, 2 * C), BF16),
-            pltpu.SemaphoreType.DMA((COLS,)),
-            pltpu.SemaphoreType.DMA((COLS,)),
-            pltpu.SemaphoreType.DMA((ROWS,)),
-            pltpu.SemaphoreType.DMA((ROWS,)),
+            pltpu.SemaphoreType.DMA((MESSAGES,)),
+            pltpu.SemaphoreType.DMA((MESSAGES,)),
             pltpu.SemaphoreType.DMA((2,)),
         ],
         compiler_params=pltpu.CompilerParams(
@@ -116,72 +212,171 @@
     )(feats, cots)
 
 
-def reduce_kernel(tgt, src, out, tgt_in, src_in, col_send, col_recv, row_send, row_recv, own):
-    row, col = greet()
-    copies = []
-    for step in range(1, COLS):
-        there = lax.rem(col + step, COLS)
-        copies.append(
-            pltpu.make_async_remote_copy(
-                src_ref=tgt.at[there],
-                dst_ref=tgt_in.at[col],
-                send_sem=col_send.at[step],
-                recv_sem=col_recv.at[step],
-                device_id={"col": there},
-                device_id_type=MESH,
-            )
+def length(bounds):
+    return bounds[1] - bounds[0]
+
+
+def reduce_kernel(tgt, src, out, *scratch):
+    send, recv = scratch[-2:]
+    row_in, row_sum, sib_in, z_in, z_out, kept = scratch[:6]
+    halves = (scratch[6:18], scratch[18:30])
+    net = Net(send, recv)
+    net.greet()
+    sib = net.push(src.at[:, 1 - net.core], sib_in, net.peer(core=1))
+
+    def toward(h, phase, sign):
+        along_x = (h == 0) == (phase == 0)
+        return net.at(x=sign) if along_x else net.at(y=sign)
+
+    def block(h, step, piece):
+        bounds = QUARTERS[2 * h + piece]
+        if h == 0:
+            return tgt.at[ring(net.x, step), :, :, span(bounds)]
+        return tgt.at[:, :, ring(net.y, step), span(bounds)]
+
+    def tail(h, piece):
+        first = QUARTERS[2 * h][0]
+        bounds = QUARTERS[2 * h + piece]
+        return pl.ds(bounds[0] - first, length(bounds))
+
+    passing = {}
+    direct = {}
+    for h in (0, 1):
+        in_p, in_m, up, um, end_p, end_m = halves[h][:6]
+        passing[h, 1] = net.push(block(h, 2, 0), in_p, toward(h, 0, 1))
+        passing[h, 3] = net.push(block(h, 2, 1), in_m, toward(h, 0, 3))
+    for h in (0, 1):
+        in_p, in_m, up, um, end_p, end_m = halves[h][:6]
+        direct[h, 1] = net.push(block(h, 1, 1), end_p.at[:, :, tail(h, 1)], toward(h, 0, 1))
+        direct[h, 3] = net.push(block(h, 3, 0), end_m.at[:, :, tail(h, 0)], toward(h, 0, 3))
+
+    sib.wait_recv()
+    for high in range(4):
+        row_sum[high] = (src[high, net.core].astype(F32) + sib_in[high].astype(F32)).astype(BF16)
+    rows = [
+        net.push(row_sum.at[ring(net.high, step)], row_in.at[net.high], net.peer(high=step))
+        for step in (2, 1, 3)
+    ]
+
+    joined = {}
+    for sign, piece in ((1, 0), (3, 1)):
+        for h in (0, 1):
+            in_p, in_m, up, um, end_p, end_m = halves[h][:6]
+            came, sums, end = (in_p, up, end_p) if sign == 1 else (in_m, um, end_m)
+            passing[h, sign].wait_recv()
+            mine = block(h, sign, piece)
+            for i in range(came.shape[0]):
+                for j in range(came.shape[1]):
+                    sums[i, j] = (came[i, j].astype(F32) + mine[i, j].astype(F32)).astype(BF16)
+            joined[h, sign] = net.push(sums, end.at[:, :, tail(h, piece)], toward(h, 0, sign))
+
+    passing_2 = {}
+    direct_2 = {}
+    for h in (0, 1):
+        in_p, in_m, up, um, end_p, end_m = halves[h][:6]
+        total, in2_p, in2_m, up2, um2, ends = halves[h][6:12]
+        for sign in (1, 3):
+            direct[h, sign].wait_recv()
+            joined[h, sign].wait_recv()
+        for i in range(end_p.shape[0]):
+            for j in range(end_p.shape[1]):
+                if h == 0:
+                    mine, to = tgt[net.x, i, j, 0:13], total.at[j, i]
+                else:
+                    mine, to = tgt[i, j, net.y, 13:25], total.at[i, j]
+                to[...] = (
+                    mine.astype(F32) + end_p[i, j].astype(F32) + end_m[i, j].astype(F32)
+                ).astype(BF16)
+        here = net.y if h == 0 else net.x
+        passing_2[h, 1] = net.push(
+            total.at[ring(here, 2), :, tail(h, 0)], in2_p, toward(h, 1, 1)
         )
-        copies[-1].start()
-    for step in range(1, ROWS):
-        there = lax.rem(row + step, ROWS)
-        copies.append(
-            pltpu.make_async_remote_copy(
-                src_ref=src.at[there],
-                dst_ref=src_in.at[row],
-                send_sem=row_send.at[step],
-                recv_sem=row_recv.at[step],
-                device_id={"row": there},
-                device_id_type=MESH,
-            )
+        passing_2[h, 3] = net.push(
+            total.at[ring(here, 2), :, tail(h, 1)], in2_m, toward(h, 1, 3)
         )
-        copies[-1].start()
-    mine = pltpu.make_async_copy(tgt.at[col], tgt_in.at[col], own.at[0])
-    also = pltpu.make_async_copy(src.at[row], src_in.at[row], own.at[1])
-    mine.start()
-    also.start()
-    mine.wait()
-    also.wait()
-    for copy in copies:
-        copy.wait()
-
-    def add(j, carry):
-        total = jnp.sum(tgt_in[:, j].astype(F32), axis=0)
-        out[j] = total + jnp.sum(src_in[:, j].astype(F32), axis=0)
-        return carry
-
-    lax.fori_loop(0, COEF, add, 0)
+        direct_2[h, 1] = net.push(
+            total.at[ring(here, 1), :, tail(h, 1)], ends.at[0, :, tail(h, 1)], toward(h, 1, 1)
+        )
+        direct_2[h, 3] = net.push(
+            total.at[ring(here, 3), :, tail(h, 0)], ends.at[1, :, tail(h, 0)], toward(h, 1, 3)
+        )
+    joined_2 = {}
+    for h in (0, 1):
+        total, in2_p, in2_m, up2, um2, ends = halves[h][6:12]
+        here = net.y if h == 0 else net.x
+        for n, (sign, piece, came, sums) in enumerate(((1, 0, in2_p, up2), (3, 1, in2_m, um2))):
+            passing_2[h, sign].wait_recv()
+            for i in range(2):
+                mine = total[ring(here, sign), i, tail(h, piece)]
+                sums[i] = (came[i].astype(F32) + mine.astype(F32)).astype(BF16)
+            joined_2[h, sign] = net.push(sums, ends.at[n, :, tail(h, piece)], toward(h, 1, sign))
+    for copy in rows:
+        copy.wait_recv()
+    across = []
+    for h in (0, 1):
+        total, in2_p, in2_m, up2, um2, ends = halves[h][6:12]
+        here = net.y if h == 0 else net.x
+        for sign in (1, 3):
+            direct_2[h, sign].wait_recv()
+            joined_2[h, sign].wait_recv()
+        at = span(HALVES[h])
+        for z_now, to in ((1 - net.z, z_out), (net.z, kept)):
+            value = total[here, z_now].astype(F32) + ends[0, z_now].astype(F32)
+            value = value + ends[1, z_now].astype(F32)
+            to[at] = value.astype(to.dtype)
+        across.append(net.push(z_out.at[at], z_in.at[at], net.at(z=1)))
+    value = kept[...] + row_sum[net.high].astype(F32)
+    for step in (1, 2, 3):
+        value = value + row_in[ring(net.high, step)].astype(F32)
+    kept[...] = value
+    for copy in across:
+        copy.wait_recv()
+    out[...] = kept[...] + z_in[...].astype(F32)
+    for copy in net.copies:
+        copy.wait_send()
 
 
 def reduce(tgt, src):
+    def buffer(*lead):
+        return pltpu.VMEM(lead + (A, C), BF16)
+
+    scratch = [
+        buffer(4, COEF),
+        buffer(4, COEF),
+        buffer(4, COEF),
+        buffer(COEF),
+        buffer(COEF),
+        pltpu.VMEM((COEF, A, C), F32),
+    ]
+    for h, lead in ((0, (2, 4)), (1, (4, 2))):
+        whole = length(HALVES[h])
+        plus, minus = length(QUARTERS[2 * h]), length(QUARTERS[2 * h + 1])
+        scratch += [
+            buffer(*lead, plus),
+            buffer(*lead, minus),
+            buffer(*lead, plus),
+            buffer(*lead, minus),
+            buffer(*lead, whole),
+            buffer(*lead, whole),
+            buffer(4, 2, whole),
+            buffer(2, plus),
+            buffer(2, minus),
+            buffer(2, plus),
+            buffer(2, minus),
+            buffer(2, 2, whole),
+        ]
     return pl.pallas_call(
         reduce_kernel,
         out_shape=jax.ShapeDtypeStruct((COEF, A, C), F32),
-        in_specs=[pl.BlockSpec(memory_space=pl.ANY)] * 2,
+        in_specs=[pl.BlockSpec(memory_space=pltpu.VMEM)] * 2,
         out_specs=pl.BlockSpec(memory_space=pltpu.VMEM),
-        scratch_shapes=[
-            pltpu.VMEM((COLS, COEF, A, C), BF16),
-            pltpu.VMEM((ROWS, COEF, A, C), BF16),
-            pltpu.SemaphoreType.DMA((COLS,)),
-            pltpu.SemaphoreType.DMA((COLS,)),
-            pltpu.SemaphoreType.DMA((ROWS,)),
-            pltpu.SemaphoreType.DMA((ROWS,)),
-            pltpu.SemaphoreType.DMA((2,)),
-        ],
+        scratch_shapes=scratch
+        + [pltpu.SemaphoreType.DMA((MESSAGES,)), pltpu.SemaphoreType.DMA((MESSAGES,))],
         compiler_params=pltpu.CompilerParams(
             collective_id=1, has_side_effects=True, vmem_limit_bytes=VMEM_LIMIT
         ),
         name="reduce_blocks",
-    )(tgt, src)
+    )(tgt.reshape(4, 2, 4, COEF, A, C), src.reshape(4, 2, COEF, A, C))
 
 
 def dot(x, y):
@@ -362,6 +557,8 @@
     feats = jnp.transpose(node_feats, (1, 0, 2))
     cots = jnp.transpose(grad_out, (1, 0, 2))
     g, s = gather(feats, cots)
+    g = g.reshape(COLS, COEF, A, 2 * C)
+    s = s.reshape(ROWS, COEF, A, C)
     tgt, src = edges(
         edge_counts, edge_src[0], edge_tgt[0], wigner[0, 0], g, s, w_zero, w_one, w_two
     )

time: 171 us -> 111 us (0.65)
  Pallas kernels: 164 us -> 105 us
    pallas_call x1, Pallas kernels: 77.9 us -> 34.9 us  [gather(): pl.pallas_call(gather_kernel, out_shape=(jax.ShapeDtypeStruct((4, 2, 4, C...]
    pallas_call x1, Pallas kernels: 40.2 us -> 24.8 us  [reduce(): pl.pallas_call(reduce_kernel, out_shape=jax.ShapeDtypeStruct((COEF, A, C)...]
where the time goes in v2:
time: 111 us; the launch traced here: 110 us
  Pallas kernels  105 us (95%)
  local copies, waits for them, and re-layouts  3.58 us (3%)
    pallas_call x1, Pallas kernels, edges(): pl.pallas_call(edge_kernel, out_shape=(jax.ShapeDtypeStruct((COLS, COEF,...  45.7 us
    pallas_call x1, Pallas kernels, gather(): pl.pallas_call(gather_kernel, out_shape=(jax.ShapeDtypeStruct((4, 2, 4, C...  34.9 us
    pallas_call x1, Pallas kernels, reduce(): pl.pallas_call(reduce_kernel, out_shape=jax.ShapeDtypeStruct((COEF, A, C)...  24.8 us
    unnamed x2, local copies, waits for them, and re-layouts  3.58 us

profile of v2, /device:TPU:2, one launch (start us, length us, event | category | flops | bytes accessed | tf_op | source)
XLA Modules:
  0.0 109.7 jit_solution(16495567542846259449)
XLA Ops:
  0.7 2.0 %copy.10 = bf16[1,1,512,475]{3,2,1,0:T(8,128)(2,1)} copy(bf16[1,1,512,475]{2,3,1,0:T(8,128)(2,1)} %param.14) | data formatting | bytes 972800 | tf_op args[5]
  2.7 34.9 %gather_blocks.1 = (bf16[4,2,4,25,8,256]{5,4,3,2,1,0:T(8,128)(2,1)}, bf16[4,2,25,8,128]{4,3,2,1,0:T(8,128)(2,1)}) custom-call(bf16[25,8,128]{2,1,0:T(8,128)(2,1)} %bitcast.14, bf16[25,8,128]{2,1,0:T(8,128)(2,1)} %bitcast.15), custom_call_target="tpu_custom_call" | custom-call | tf_op jit(solution)/shard_map/gather_blocks/pallas_call | solution.py:194
  37.6 45.7 %edge_gradients.1 = (bf16[32,25,8,128]{3,2,1,0:T(8,128)(2,1)}, bf16[8,25,8,128]{3,2,1,0:T(8,128)(2,1)}) custom-call(s32[1,1]{1,0:T(1,128)S(6)} %copy.12.count, s32[1,512]{1,0:T(1,128)} %bitcast.18, s32[1,512]{1,0:T(1,128)} %bitcast.19, bf16[512,475]{1,0:T(8,128)(2,1)} %bitcast.11, bf16[32,25,8,256]{3,2,1,0:T(8,128)(2,1)} %bitcast.16, ...), custom_call_target="tpu_custom_call" | custom-call | flops 12000000000 | bytes 12000000 | tf_op jit(solution)/shard_map/edge_gradients/pallas_call | solution.py:527
  83.4 24.8 %reduce_blocks.1 = f32[25,8,128]{2,1,0:T(8,128)} custom-call(bf16[4,2,4,25,8,128]{5,4,3,2,1,0:T(8,128)(2,1)} %bitcast.10, bf16[4,2,25,8,128]{4,3,2,1,0:T(8,128)(2,1)} %bitcast.12), custom_call_target="tpu_custom_call" | custom-call | tf_op jit(solution)/shard_map/reduce_blocks/pallas_call | solution.py:368
  108.2 1.5 %copy.13 = f32[8,25,128]{2,0,1:T(8,128)} copy(f32[8,25,128]{2,0,1:T(8,128)} %bitcast.13) | data formatting | bytes 204800

commit v3 on v2

v3 whole, which is shorter than its diff:
```python
import jax
import jax.numpy as jnp
from jax import lax
from jax.experimental import pallas as pl
from jax.experimental.pallas import tpu as pltpu
from jax.sharding import PartitionSpec as P

MESH = pl.DeviceIdType.MESH
F32 = jnp.float32
BF16 = jnp.bfloat16

ROWS = 8
COLS = 32
A = 8
E = 512
C = 128
COEF = 25
PAIRS = 13
FRAME = 19
GROUP = 16
BLOCK = 256
TGT = COLS * A
SRC = ROWS * A
VMEM_LIMIT = 58 * 1024 * 1024


def frame_rows(degree):
    rows = [degree]
    if degree >= 1:
        rows += [5 + degree - 1, 9 + degree - 1]
    if degree >= 2:
        rows += [13 + degree - 2, 16 + degree - 2]
    return rows


def degree_cols(degree):
    return list(range(degree * degree, (degree + 1) * (degree + 1)))


def ring(value, step):
    return lax.rem(value + step, 4)


class Net:
    def __init__(self, send, recv):
        row = lax.axis_index("row")
        col = lax.axis_index("col")
        self.x = lax.div(col, 8)
        self.z = lax.rem(lax.div(col, 4), 2)
        self.y = lax.rem(col, 4)
        self.high = lax.div(row, 2)
        self.core = lax.rem(row, 2)
        self.send = send
        self.recv = recv
        self.copies = []

    def at(self, x=0, z=0, y=0):
        z_now = 1 - self.z if z else self.z
        return {"col": ring(self.x, x) * 8 + z_now * 4 + ring(self.y, y)}

    def peer(self, high=0, core=0):
        core_now = 1 - self.core if core else self.core
        return {"row": ring(self.high, high) * 2 + core_now}

    def greet(self):
        barrier = pltpu.get_barrier_semaphore()
        devices = [self.at(x=1), self.at(x=3), self.at(y=1), self.at(y=3), self.at(z=1)]
        devices += [self.peer(high=step) for step in (1, 2, 3)] + [self.peer(core=1)]
        for device in devices:
            pl.semaphore_signal(barrier, inc=1, device_id=device, device_id_type=MESH)
        pl.semaphore_wait(barrier, len(devices))

    def push(self, source, target, device):
        n = len(self.copies)
        copy = pltpu.make_async_remote_copy(
            src_ref=source,
            dst_ref=target,
            send_sem=self.send.at[n],
            recv_sem=self.recv.at[n],
            device_id=device,
            device_id_type=MESH,
        )
        copy.start()
        self.copies.append(copy)
        return copy


QUARTERS = ((0, 7), (7, 13), (13, 19), (19, 25))
HALVES = ((0, 13), (13, 25))
MESSAGES = 160


def span(bounds):
    return pl.ds(bounds[0], bounds[1] - bounds[0])


def length(bounds):
    return bounds[1] - bounds[0]


def reduce_body(net, sib, tgt, src, out, scratch):
    row_in, row_sum, sib_in, z_in, z_out, kept = scratch[:6]
    halves = (scratch[6:18], scratch[18:30])

    def toward(h, phase, sign):
        along_x = (h == 0) == (phase == 0)
        return net.at(x=sign) if along_x else net.at(y=sign)

    def block(h, step, piece):
        bounds = QUARTERS[2 * h + piece]
        if h == 0:
            return tgt.at[ring(net.x, step), :, :, span(bounds)]
        return tgt.at[:, :, ring(net.y, step), span(bounds)]

    def tail(h, piece):
        first = QUARTERS[2 * h][0]
        bounds = QUARTERS[2 * h + piece]
        return pl.ds(bounds[0] - first, length(bounds))

    passing = {}
    direct = {}
    for h in (0, 1):
        in_p, in_m, up, um, end_p, end_m = halves[h][:6]
        passing[h, 1] = net.push(block(h, 2, 0), in_p, toward(h, 0, 1))
        passing[h, 3] = net.push(block(h, 2, 1), in_m, toward(h, 0, 3))
    for h in (0, 1):
        in_p, in_m, up, um, end_p, end_m = halves[h][:6]
        direct[h, 1] = net.push(block(h, 1, 1), end_p.at[:, :, tail(h, 1)], toward(h, 0, 1))
        direct[h, 3] = net.push(block(h, 3, 0), end_m.at[:, :, tail(h, 0)], toward(h, 0, 3))

    sib.wait_recv()
    for high in range(4):
        row_sum[high] = (src[high, net.core].astype(F32) + sib_in[high].astype(F32)).astype(BF16)
    rows = [
        net.push(row_sum.at[ring(net.high, step)], row_in.at[net.high], net.peer(high=step))
        for step in (2, 1, 3)
    ]

    joined = {}
    for sign, piece in ((1, 0), (3, 1)):
        for h in (0, 1):
            in_p, in_m, up, um, end_p, end_m = halves[h][:6]
            came, sums, end = (in_p, up, end_p) if sign == 1 else (in_m, um, end_m)
            passing[h, sign].wait_recv()
            mine = block(h, sign, piece)
            for i in range(came.shape[0]):
                for j in range(came.shape[1]):
                    sums[i, j] = (came[i, j].astype(F32) + mine[i, j].astype(F32)).astype(BF16)
            joined[h, sign] = net.push(sums, end.at[:, :, tail(h, piece)], toward(h, 0, sign))

    passing_2 = {}
    direct_2 = {}
    for h in (0, 1):
        in_p, in_m, up, um, end_p, end_m = halves[h][:6]
        total, in2_p, in2_m, up2, um2, ends = halves[h][6:12]
        for sign in (1, 3):
            direct[h, sign].wait_recv()
            joined[h, sign].wait_recv()
        for i in range(end_p.shape[0]):
            for j in range(end_p.shape[1]):
                if h == 0:
                    mine, to = tgt[net.x, i, j, 0:13], total.at[j, i]
                else:
                    mine, to = tgt[i, j, net.y, 13:25], total.at[i, j]
                to[...] = (
                    mine.astype(F32) + end_p[i, j].astype(F32) + end_m[i, j].astype(F32)
                ).astype(BF16)
        here = net.y if h == 0 else net.x
        passing_2[h, 1] = net.push(
            total.at[ring(here, 2), :, tail(h, 0)], in2_p, toward(h, 1, 1)
        )
        passing_2[h, 3] = net.push(
            total.at[ring(here, 2), :, tail(h, 1)], in2_m, toward(h, 1, 3)
        )
        direct_2[h, 1] = net.push(
            total.at[ring(here, 1), :, tail(h, 1)], ends.at[0, :, tail(h, 1)], toward(h, 1, 1)
        )
        direct_2[h, 3] = net.push(
            total.at[ring(here, 3), :, tail(h, 0)], ends.at[1, :, tail(h, 0)], toward(h, 1, 3)
        )
    joined_2 = {}
    for h in (0, 1):
        total, in2_p, in2_m, up2, um2, ends = halves[h][6:12]
        here = net.y if h == 0 else net.x
        for n, (sign, piece, came, sums) in enumerate(((1, 0, in2_p, up2), (3, 1, in2_m, um2))):
            passing_2[h, sign].wait_recv()
            for i in range(2):
                mine = total[ring(here, sign), i, tail(h, piece)]
                sums[i] = (came[i].astype(F32) + mine.astype(F32)).astype(BF16)
            joined_2[h, sign] = net.push(sums, ends.at[n, :, tail(h, piece)], toward(h, 1, sign))
    for copy in rows:
        copy.wait_recv()
    across = []
    for h in (0, 1):
        total, in2_p, in2_m, up2, um2, ends = halves[h][6:12]
        here = net.y if h == 0 else net.x
        for sign in (1, 3):
            direct_2[h, sign].wait_recv()
            joined_2[h, sign].wait_recv()
        at = span(HALVES[h])
        for z_now, to in ((1 - net.z, z_out), (net.z, kept)):
            value = total[here, z_now].astype(F32) + ends[0, z_now].astype(F32)
            value = value + ends[1, z_now].astype(F32)
            to[at] = value.astype(to.dtype)
        across.append(net.push(z_out.at[at], z_in.at[at], net.at(z=1)))
    value = kept[...] + row_sum[net.high].astype(F32)
    for step in (1, 2, 3):
        value = value + row_in[ring(net.high, step)].astype(F32)
    kept[...] = value
    for copy in across:
        copy.wait_recv()
    out[...] = kept[...] + z_in[...].astype(F32)


class Flow:
    def __init__(self, net, own, full):
        self.net = net
        self.own = own
        self.full = full
        self.inner = {}
        self.outer = {}
        self.passed = {}
        self.last = []

    def place(self, h, outer, inner, z, bounds):
        net = self.net
        near, far = (inner, outer) if h == 0 else (outer, inner)
        z_now = (net.z, 1 - net.z, slice(0, 2))[z]
        return self.full.at[ring(net.x, far), z_now, ring(net.y, near), span(bounds)]

    def step_to(self, h, phase, sign):
        along_y = (h == 0) == (phase == 0)
        return self.net.at(y=sign) if along_y else self.net.at(x=sign)

    def spread(self, h, inner, z):
        block = self.place(h, 0, inner, z, HALVES[h])
        source = self.own.at[span(HALVES[h])] if (inner, z) == (0, 0) else block
        for sign in (1, 3):
            self.outer[h, z, inner, sign] = self.net.push(source, block, self.step_to(h, 1, sign))

    def relay(self, h, z, inner):
        for sign, quarter in ((1, 0), (3, 1)):
            self.outer[h, z, inner, sign].wait_recv()
            block = self.place(h, 4 - sign, inner, z, QUARTERS[2 * h + quarter])
            self.last.append(self.net.push(block, block, self.step_to(h, 1, sign)))

    def send_own(self):
        net = self.net
        self.across = net.push(self.own, self.full.at[net.x, net.z, net.y], net.at(z=1))
        for h in (0, 1):
            for sign in (1, 3):
                self.inner[h, 0, sign] = net.push(
                    self.own.at[span(HALVES[h])],
                    self.place(h, 0, 0, 0, HALVES[h]),
                    self.step_to(h, 0, sign),
                )
        for h in (0, 1):
            self.spread(h, 0, 0)

    def send_partner(self):
        self.across.wait_recv()
        for h in (0, 1):
            block = self.place(h, 0, 0, 1, HALVES[h])
            for sign in (1, 3):
                self.inner[h, 1, sign] = self.net.push(block, block, self.step_to(h, 0, sign))
        for h in (0, 1):
            self.spread(h, 0, 1)

    def pass_on(self):
        for sign, quarter in ((1, 0), (3, 1)):
            for h in (0, 1):
                self.inner[h, 0, sign].wait_recv()
                self.inner[h, 1, sign].wait_recv()
                block = self.place(h, 0, 4 - sign, 2, QUARTERS[2 * h + quarter])
                self.passed[h, sign] = self.net.push(block, block, self.step_to(h, 0, sign))
                self.spread(h, 4 - sign, 2)

    def relay_first(self):
        for z in (0, 1):
            for h in (0, 1):
                self.relay(h, z, 0)

    def spread_far(self):
        for h in (0, 1):
            self.passed[h, 1].wait_recv()
            self.passed[h, 3].wait_recv()
            self.spread(h, 2, 2)

    def relay_rest(self, inner):
        for h in (0, 1):
            self.relay(h, 2, inner)

    def finish(self):
        for copy in self.last:
            copy.wait_recv()


def dot(x, y):
    return jnp.dot(x, y, preferred_element_type=F32)


def dot_t(x, y):
    return lax.dot_general(x, y, (((1,), (1,)), ((), ())), preferred_element_type=F32)


def half(j):
    return slice((j % 2) * C, (j % 2) * C + C)


def hot(ids, size, axis):
    return (ids == lax.broadcasted_iota(jnp.int32, size, axis)).astype(F32).astype(BF16)


def fused_kernel(
    count, src_ids, tgt_ids, rot, feats, cots, w0, w1, w2, out,
    gf, gc, gs, w0_in, full1, full2, turn, hot_t, hot_s, back_t, back_s,
    xf, xc, xs, frame, grad_y, y, tgt_sum, src_sum, local_sem, send, recv, *reduce_scratch,
):
    net = Net(send, recv)
    loads = [pltpu.make_async_copy(w0, w0_in, local_sem.at[0])]
    for n, (weights, full) in enumerate(((w1, full1), (w2, full2))):
        k, m = weights.shape[1:]
        for i in range(2):
            for j in range(2):
                loads.append(
                    pltpu.make_async_copy(
                        weights.at[(i + j) % 2],
                        full.at[pl.ds(i * k, k), pl.ds(j * m, m)],
                        local_sem.at[1 + 4 * n + 2 * i + j],
                    )
                )
    mine = [
        pltpu.make_async_copy(feats, gf.at[net.x, net.z, net.y], local_sem.at[9]),
        pltpu.make_async_copy(cots, gc.at[net.x, net.z, net.y], local_sem.at[10]),
        pltpu.make_async_copy(feats, gs.at[net.high, net.core], local_sem.at[11]),
    ]
    for copy in mine + loads:
        copy.start()
    net.greet()

    first = Flow(net, feats, gf)
    second = Flow(net, cots, gc)
    first.send_own()
    sibling = [net.push(feats, gs.at[net.high, net.core], net.peer(core=1))]
    rows = [net.push(feats, gs.at[net.high, net.core], net.peer(high=step)) for step in (1, 3, 2)]

    tgt_row = tgt_ids[...]
    src_row = src_ids[...]
    tgt_col = jnp.transpose(jnp.broadcast_to(tgt_row, (C, E)))
    src_col = jnp.transpose(jnp.broadcast_to(src_row, (C, E)))
    hot_t[:, 0:C] = hot(tgt_col, (E, C), 1)
    hot_t[:, C : 2 * C] = hot(tgt_col - C, (E, C), 1)
    hot_s[...] = hot(src_col, (E, C), 1)[:, 0:SRC]
    first.send_partner()
    valid = lax.broadcasted_iota(jnp.int32, (1, E), 1) < count[0, 0]
    back_t[...] = hot(jnp.where(valid, tgt_row, -1), (TGT, E), 0)
    back_s[...] = hot(jnp.where(valid, src_row, -1), (SRC, E), 0)
    first.pass_on()
    identity = hot(lax.broadcasted_iota(jnp.int32, (E, E), 0), (E, E), 1)
    turn[...] = dot_t(identity, rot[...])
    first.relay_first()
    first.spread_far()
    for step, copy in zip((1, 3, 2), rows):
        copy.wait_recv()
        block = gs.at[ring(net.high, 4 - step), net.core]
        sibling.append(net.push(block, block, net.peer(core=1)))
    second.send_own()
    first.relay_rest(3)
    first.relay_rest(1)
    first.relay_rest(2)
    second.send_partner()
    for copy in mine + loads:
        copy.wait()
    for weights, full in ((w1, full1), (w2, full2)):
        k, m = weights.shape[1:]
        full[k : 2 * k, 0:m] = -full[k : 2 * k, 0:m]
    for copy in sibling:
        copy.wait_recv()

    def pair_of(full, p, rows):
        both = []
        for j in (2 * p, jnp.minimum(2 * p + 1, COEF - 1)):
            piece = full[:, :, :, j] if full.ndim == 6 else full[:, :, j]
            both.append(piece.astype(F32).reshape(rows, C))
        return jnp.concatenate(both, axis=1).astype(BF16)

    def gather_some(items, start, stop):
        def body(p, carry):
            for marks, full, rows, to in items:
                to[p] = dot(marks[...], pair_of(full, p, rows)).astype(BF16)
            return carry

        lax.fori_loop(start, stop, body, 0)

    gather_some(((hot_s, gs, SRC, xs),), 0, PAIRS)
    second.pass_on()
    first.finish()
    second.relay_first()
    gather_some(((hot_t, gf, TGT, xf),), 0, PAIRS)
    second.spread_far()

    def factor_of(matrix, entry):
        return jnp.broadcast_to(matrix[:, entry : entry + 1], (GROUP, C))

    def rotate(i, carry):
        at = pl.ds(pl.multiple_of(i * GROUP, GROUP), GROUP)
        matrix = turn[at, :]
        for degree in range(5):
            cols = degree_cols(degree)
            from_src = [xs[j // 2, at, half(j)].astype(F32) for j in cols]
            from_tgt = [xf[j // 2, at, half(j)].astype(F32) for j in cols]
            for k in frame_rows(degree):
                sums = [None, None]
                for n, j in enumerate(cols):
                    factor = factor_of(matrix, k * COEF + j)
                    for which, values in enumerate((from_src, from_tgt)):
                        term = factor * values[n]
                        sums[which] = term if sums[which] is None else sums[which] + term
                frame[at, 2 * k * C : (2 * k + 1) * C] = sums[0].astype(BF16)
                frame[at, (2 * k + 1) * C : (2 * k + 2) * C] = sums[1].astype(BF16)
        return carry

    steps = E // GROUP
    lax.fori_loop(0, steps // 4, rotate, 0)
    second.relay_rest(3)
    second.relay_rest(1)
    lax.fori_loop(steps // 4, steps // 2, rotate, 0)
    second.relay_rest(2)
    lax.fori_loop(steps // 2, steps, rotate, 0)

    parts = ((0, 5, w0_in), (5, 8, full1), (13, 6, full2))

    def forward(i, carry):
        at = pl.ds(pl.multiple_of(i * BLOCK, BLOCK), BLOCK)
        for begin, rows, weights in parts:
            y[at, begin * C : (begin + rows) * C] = dot(
                frame[at, 2 * begin * C : 2 * (begin + rows) * C], weights[...]
            )
        return carry

    lax.fori_loop(0, E // BLOCK, forward, 0)
    second.finish()
    gather_some(((hot_t, gc, TGT, xc),), 0, PAIRS)

    def gate(i, carry):
        at = pl.ds(pl.multiple_of(i * GROUP, GROUP), GROUP)
        matrix = turn[at, :]
        scalar = y[at, 0:C]
        gating = jax.nn.sigmoid(scalar)
        slope = gating * (1.0 - gating)
        total = jnp.zeros((GROUP, C), F32)
        lowest = None
        for degree in range(5):
            cols = degree_cols(degree)
            values = [xc[j // 2, at, half(j)].astype(F32) for j in cols]
            for k in frame_rows(degree):
                value = None
                for n, j in enumerate(cols):
                    term = factor_of(matrix, k * COEF + j) * values[n]
                    value = term if value is None else value + term
                if k == 0:
                    lowest = value
                else:
                    total = total + value * y[at, k * C : (k + 1) * C]
                    grad_y[at, k * C : (k + 1) * C] = (gating * value).astype(BF16)
        grad_y[at, 0:C] = (lowest * (gating + scalar * slope) + total * slope).astype(BF16)
        return carry

    lax.fori_loop(0, steps, gate, 0)

    def backward(i, carry):
        at = pl.ds(pl.multiple_of(i * BLOCK, BLOCK), BLOCK)
        for begin, rows, weights in parts:
            frame[at, 2 * begin * C : 2 * (begin + rows) * C] = dot_t(
                grad_y[at, begin * C : (begin + rows) * C], weights[...]
            ).astype(BF16)
        return carry

    lax.fori_loop(0, E // BLOCK, backward, 0)

    def unrotate(i, carry):
        at = pl.ds(pl.multiple_of(i * GROUP, GROUP), GROUP)
        matrix = turn[at, :]
        for degree in range(5):
            rows = frame_rows(degree)
            of_src = [frame[at, 2 * k * C : (2 * k + 1) * C].astype(F32) for k in rows]
            of_tgt = [frame[at, (2 * k + 1) * C : (2 * k + 2) * C].astype(F32) for k in rows]
            for j in degree_cols(degree):
                sums = [None, None]
                for n, k in enumerate(rows):
                    factor = factor_of(matrix, k * COEF + j)
                    for which, values in enumerate((of_src, of_tgt)):
                        term = factor * values[n]
                        sums[which] = term if sums[which] is None else sums[which] + term
                xs[j // 2, at, half(j)] = sums[0].astype(BF16)
                xf[j // 2, at, half(j)] = sums[1].astype(BF16)
        return carry

    lax.fori_loop(0, steps, unrotate, 0)

    def scatter(marks, grads, to, lead):
        for p in range(PAIRS):
            both = dot(marks[...], grads[p])
            for j in (2 * p, 2 * p + 1):
                if j < COEF:
                    value = both[:, half(j)].reshape(lead + (A, C)).astype(BF16)
                    if len(lead) == 3:
                        to[:, :, :, j] = value
                    else:
                        to[:, :, j] = value

    scatter(back_s, xs, src_sum, (4, 2))
    sib = net.push(src_sum.at[:, 1 - net.core], reduce_scratch[2], net.peer(core=1))
    scatter(back_t, xf, tgt_sum, (4, 2, 4))
    reduce_body(net, sib, tgt_sum, src_sum, out, reduce_scratch)
    for copy in net.copies:
        copy.wait_send()


def fused(count, src_ids, tgt_ids, rot, feats, cots, w0, w1, w2):
    def buffer(*lead):
        return pltpu.VMEM(lead + (A, C), BF16)

    scratch = [
        buffer(4, 2, 4, COEF),
        buffer(4, 2, 4, COEF),
        buffer(4, 2, COEF),
        pltpu.VMEM(w0.shape, BF16),
        pltpu.VMEM((2 * w1.shape[1], 2 * w1.shape[2]), BF16),
        pltpu.VMEM((2 * w2.shape[1], 2 * w2.shape[2]), BF16),
        pltpu.VMEM((E, FRAME * COEF), F32),
        pltpu.VMEM((E, TGT), BF16),
        pltpu.VMEM((E, SRC), BF16),
        pltpu.VMEM((TGT, E), BF16),
        pltpu.VMEM((SRC, E), BF16),
        pltpu.VMEM((PAIRS, E, 2 * C), BF16),
        pltpu.VMEM((PAIRS, E, 2 * C), BF16),
        pltpu.VMEM((PAIRS, E, 2 * C), BF16),
        pltpu.VMEM((E, FRAME * 2 * C), BF16),
        pltpu.VMEM((E, FRAME * C), BF16),
        pltpu.VMEM((E, FRAME * C), F32),
        buffer(4, 2, 4, COEF),
        buffer(4, 2, COEF),
        pltpu.SemaphoreType.DMA((12,)),
        pltpu.SemaphoreType.DMA((MESSAGES,)),
        pltpu.SemaphoreType.DMA((MESSAGES,)),
        buffer(4, COEF),
        buffer(4, COEF),
        buffer(4, COEF),
        buffer(COEF),
        buffer(COEF),
        pltpu.VMEM((COEF, A, C), F32),
    ]
    for h, lead in ((0, (2, 4)), (1, (4, 2))):
        whole = length(HALVES[h])
        plus, minus = length(QUARTERS[2 * h]), length(QUARTERS[2 * h + 1])
        scratch += [
            buffer(*lead, plus),
            buffer(*lead, minus),
            buffer(*lead, plus),
            buffer(*lead, minus),
            buffer(*lead, whole),
            buffer(*lead, whole),
            buffer(4, 2, whole),
            buffer(2, plus),
            buffer(2, minus),
            buffer(2, plus),
            buffer(2, minus),
            buffer(2, 2, whole),
        ]
    vmem = pl.BlockSpec(memory_space=pltpu.VMEM)
    hbm = pl.BlockSpec(memory_space=pl.ANY)
    return pl.pallas_call(
        fused_kernel,
        out_shape=jax.ShapeDtypeStruct((COEF, A, C), F32),
        in_specs=[pl.BlockSpec(memory_space=pltpu.SMEM)] + [vmem] * 5 + [hbm] * 3,
        out_specs=vmem,
        scratch_shapes=scratch,
        compiler_params=pltpu.CompilerParams(
            collective_id=0, has_side_effects=True, vmem_limit_bytes=VMEM_LIMIT
        ),
        name="edge_gradients",
    )(count, src_ids, tgt_ids, rot, feats, cots, w0, w1, w2)


def local(node_feats, grad_out, edge_src, edge_tgt, edge_counts, wigner, w_zero, w_one, w_two):
    total = fused(
        edge_counts,
        edge_src[0],
        edge_tgt[0],
        jnp.transpose(wigner[0, 0]),
        jnp.transpose(node_feats, (1, 0, 2)),
        jnp.transpose(grad_out, (1, 0, 2)),
        w_zero,
        w_one,
        w_two,
    )
    return jnp.transpose(total, (1, 0, 2))


def solution(mesh):
    placed = (
        P(("row", "col"), None, None),
        P(("row", "col"), None, None),
        P("row", "col", None),
        P("row", "col", None),
        P("row", "col"),
        P("row", "col", None, None),
        P(),
        P(),
        P(),
    )
    return jax.shard_map(
        local, mesh=mesh, in_specs=placed, out_specs=P(("row", "col"), None, None), check_vma=False
    )
```

time: 111 us -> 118 us (1.063); the launches traced: 110 us -> 118 us
  Pallas kernels: 105 us -> 116 us
  local copies, waits for them, and re-layouts: 3.58 us -> 1.54 us
    pallas_call x3 -> x1, Pallas kernels: 105 us -> 116 us  [fused(): pl.pallas_call(fused_kernel, out_shape=jax.ShapeDtypeStruct((COEF, A, C),...]
    unnamed x2 -> x1, local copies, waits for them, and re-layouts: 3.58 us -> 1.54 us
where the time goes in v3:
time: 118 us
  Pallas kernels  116 us (98%)
  local copies, waits for them, and re-layouts  1.54 us (1%)
    pallas_call x1, Pallas kernels, fused(): pl.pallas_call(fused_kernel, out_shape=jax.ShapeDtypeStruct((COEF, A, C),...  116 us

profile of v3, /device:TPU:2, one launch (start us, length us, event | category | flops | bytes accessed | tf_op | source)
XLA Modules:
  0.0 118.2 jit_solution(1438873465209055470)
XLA Ops:
  0.7 116.0 %edge_gradients.1 = f32[25,8,128]{2,1,0:T(8,128)} custom-call(s32[1,1]{1,0:T(1,128)S(6)} %copy.11.count, s32[1,512]{1,0:T(1,128)} %bitcast.12, s32[1,512]{1,0:T(1,128)} %bitcast.13, bf16[475,512]{1,0:T(8,128)(2,1)} %bitcast.8, bf16[25,8,128]{2,1,0:T(8,128)(2,1)} %bitcast.10, bf16[25,8,128]{2,1,0:T(8,128)(2,1)} %bitcast.11, bf16[1280,640]{1,0:T(8,128)(2,1)} %w0.1, ...), custom_call_target="tpu_custom_call" | custom-call | tf_op jit(solution)/shard_map/edge_gradients/pallas_call | solution.py:573
  116.7 1.5 %copy.12 = f32[8,25,128]{2,0,1:T(8,128)} copy(f32[8,25,128]{2,0,1:T(8,128)} %bitcast.9) | data formatting | bytes 204800

commit v4 on v3

--- a/solution.py
+++ b/solution.py
@@ -19,6 +19,7 @@
 FRAME = 19
 GROUP = 16
 BLOCK = 256
+LANES = 128
 TGT = COLS * A
 SRC = ROWS * A
 VMEM_LIMIT = 58 * 1024 * 1024
@@ -303,17 +304,31 @@
     return lax.dot_general(x, y, (((1,), (1,)), ((), ())), preferred_element_type=F32)
 
 
-def half(j):
-    return slice((j % 2) * C, (j % 2) * C + C)
-
-
-def hot(ids, size, axis):
-    return (ids == lax.broadcasted_iota(jnp.int32, size, axis)).astype(F32).astype(BF16)
+def t_dot(x, y):
+    return lax.dot_general(x, y, (((0,), (0,)), ((), ())), preferred_element_type=F32)
+
+
+def flip(value):
+    return jnp.transpose(value.astype(F32)).astype(BF16)
+
+
+def hot(ids, size):
+    return (ids == lax.broadcasted_iota(jnp.int32, size, 0)).astype(F32).astype(BF16)
+
+
+def tile_at(i):
+    lanes = pl.ds(pl.multiple_of(lax.div(i, C // GROUP) * LANES, LANES), LANES)
+    shift = lax.rem(i, C // GROUP) * GROUP
+
+    def rows(block):
+        return pl.ds(pl.multiple_of(block * C + shift, GROUP), GROUP)
+
+    return lanes, rows
 
 
 def fused_kernel(
     count, src_ids, tgt_ids, rot, feats, cots, w0, w1, w2, out,
-    gf, gc, gs, w0_in, full1, full2, turn, hot_t, hot_s, back_t, back_s,
+    gf, gc, gs, w0_in, full1, full2, w0_flip, flip1, flip2, rot_wide, mark_t, mark_s,
     xf, xc, xs, frame, grad_y, y, tgt_sum, src_sum, local_sem, send, recv, *reduce_scratch,
 ):
     net = Net(send, recv)
@@ -344,20 +359,38 @@
     sibling = [net.push(feats, gs.at[net.high, net.core], net.peer(core=1))]
     rows = [net.push(feats, gs.at[net.high, net.core], net.peer(high=step)) for step in (1, 3, 2)]
 
-    tgt_row = tgt_ids[...]
-    src_row = src_ids[...]
-    tgt_col = jnp.transpose(jnp.broadcast_to(tgt_row, (C, E)))
-    src_col = jnp.transpose(jnp.broadcast_to(src_row, (C, E)))
-    hot_t[:, 0:C] = hot(tgt_col, (E, C), 1)
-    hot_t[:, C : 2 * C] = hot(tgt_col - C, (E, C), 1)
-    hot_s[...] = hot(src_col, (E, C), 1)[:, 0:SRC]
+    valid = lax.broadcasted_iota(jnp.int32, (1, E), 1) < count[0, 0]
+    mark_t[...] = hot(jnp.where(valid, tgt_ids[...], -1), (TGT, E))
+    mark_s[...] = hot(jnp.where(valid, src_ids[...], -1), (SRC, E))
     first.send_partner()
-    valid = lax.broadcasted_iota(jnp.int32, (1, E), 1) < count[0, 0]
-    back_t[...] = hot(jnp.where(valid, tgt_row, -1), (TGT, E), 0)
-    back_s[...] = hot(jnp.where(valid, src_row, -1), (SRC, E), 0)
+    rot_wide[...] = rot[...].astype(F32)
+    for copy in mine + loads:
+        copy.wait()
+
+    def flip_zero(r, carry):
+        at = pl.ds(pl.multiple_of(r * BLOCK, BLOCK), BLOCK)
+        w0_flip[:, at] = flip(w0_in[at, :])
+        return carry
+
+    lax.fori_loop(0, w0.shape[0] // BLOCK, flip_zero, 0)
     first.pass_on()
-    identity = hot(lax.broadcasted_iota(jnp.int32, (E, E), 0), (E, E), 1)
-    turn[...] = dot_t(identity, rot[...])
+
+    def flip_order(weights, full, full_flip):
+        k, m = weights.shape[1:]
+
+        def body(r, carry):
+            at = pl.ds(pl.multiple_of(r * BLOCK, BLOCK), BLOCK)
+            below = pl.ds(pl.multiple_of(r * BLOCK + k, BLOCK), BLOCK)
+            full[below, 0:m] = -full[below, 0:m]
+            for j in range(2):
+                value = flip(full[at, j * m : (j + 1) * m])
+                full_flip[j * m : (j + 1) * m, at] = value
+                full_flip[(1 - j) * m : (2 - j) * m, below] = -value if j else value
+            return carry
+
+        lax.fori_loop(0, k // BLOCK, body, 0)
+
+    flip_order(w1, full1, flip1)
     first.relay_first()
     first.spread_far()
     for step, copy in zip((1, 3, 2), rows):
@@ -367,60 +400,55 @@
     second.send_own()
     first.relay_rest(3)
     first.relay_rest(1)
+    flip_order(w2, full2, flip2)
     first.relay_rest(2)
     second.send_partner()
-    for copy in mine + loads:
-        copy.wait()
-    for weights, full in ((w1, full1), (w2, full2)):
-        k, m = weights.shape[1:]
-        full[k : 2 * k, 0:m] = -full[k : 2 * k, 0:m]
     for copy in sibling:
         copy.wait_recv()
 
     def pair_of(full, p, rows):
         both = []
         for j in (2 * p, jnp.minimum(2 * p + 1, COEF - 1)):
-            piece = full[:, :, :, j] if full.ndim == 6 else full[:, :, j]
+            piece = full[:, :, :, j] if len(full.shape) == 6 else full[:, :, j]
             both.append(piece.astype(F32).reshape(rows, C))
         return jnp.concatenate(both, axis=1).astype(BF16)
 
-    def gather_some(items, start, stop):
+    def gather_some(marks, full, rows, to):
         def body(p, carry):
-            for marks, full, rows, to in items:
-                to[p] = dot(marks[...], pair_of(full, p, rows)).astype(BF16)
+            at = pl.ds(pl.multiple_of(p * 2 * C, 2 * C), 2 * C)
+            to[at, :] = t_dot(pair_of(full, p, rows), marks[...]).astype(BF16)
             return carry
 
-        lax.fori_loop(start, stop, body, 0)
-
-    gather_some(((hot_s, gs, SRC, xs),), 0, PAIRS)
+        lax.fori_loop(0, PAIRS, body, 0)
+
+    gather_some(mark_s, gs, SRC, xs)
     second.pass_on()
     first.finish()
     second.relay_first()
-    gather_some(((hot_t, gf, TGT, xf),), 0, PAIRS)
+    gather_some(mark_t, gf, TGT, xf)
     second.spread_far()
 
-    def factor_of(matrix, entry):
-        return jnp.broadcast_to(matrix[:, entry : entry + 1], (GROUP, C))
+    def factor_of(entry, lanes):
+        return jnp.broadcast_to(rot_wide[entry : entry + 1, lanes], (GROUP, LANES))
 
     def rotate(i, carry):
-        at = pl.ds(pl.multiple_of(i * GROUP, GROUP), GROUP)
-        matrix = turn[at, :]
+        lanes, rows = tile_at(i)
         for degree in range(5):
             cols = degree_cols(degree)
-            from_src = [xs[j // 2, at, half(j)].astype(F32) for j in cols]
-            from_tgt = [xf[j // 2, at, half(j)].astype(F32) for j in cols]
+            from_src = [xs[rows(j), lanes].astype(F32) for j in cols]
+            from_tgt = [xf[rows(j), lanes].astype(F32) for j in cols]
             for k in frame_rows(degree):
                 sums = [None, None]
                 for n, j in enumerate(cols):
-                    factor = factor_of(matrix, k * COEF + j)
+                    factor = factor_of(k * COEF + j, lanes)
                     for which, values in enumerate((from_src, from_tgt)):
                         term = factor * values[n]
                         sums[which] = term if sums[which] is None else sums[which] + term
-                frame[at, 2 * k * C : (2 * k + 1) * C] = sums[0].astype(BF16)
-                frame[at, (2 * k + 1) * C : (2 * k + 2) * C] = sums[1].astype(BF16)
+                frame[rows(2 * k), lanes] = sums[0].astype(BF16)
+                frame[rows(2 * k + 1), lanes] = sums[1].astype(BF16)
         return carry
 
-    steps = E // GROUP
+    steps = (E // LANES) * (C // GROUP)
     lax.fori_loop(0, steps // 4, rotate, 0)
     second.relay_rest(3)
     second.relay_rest(1)
@@ -428,90 +456,87 @@
     second.relay_rest(2)
     lax.fori_loop(steps // 2, steps, rotate, 0)
 
-    parts = ((0, 5, w0_in), (5, 8, full1), (13, 6, full2))
-
     def forward(i, carry):
         at = pl.ds(pl.multiple_of(i * BLOCK, BLOCK), BLOCK)
-        for begin, rows, weights in parts:
-            y[at, begin * C : (begin + rows) * C] = dot(
-                frame[at, 2 * begin * C : 2 * (begin + rows) * C], weights[...]
+        for begin, rows, weights in ((0, 5, w0_flip), (5, 8, flip1), (13, 6, flip2)):
+            y[begin * C : (begin + rows) * C, at] = dot(
+                weights[...], frame[2 * begin * C : 2 * (begin + rows) * C, at]
             )
         return carry
 
     lax.fori_loop(0, E // BLOCK, forward, 0)
     second.finish()
-    gather_some(((hot_t, gc, TGT, xc),), 0, PAIRS)
+    gather_some(mark_t, gc, TGT, xc)
 
     def gate(i, carry):
-        at = pl.ds(pl.multiple_of(i * GROUP, GROUP), GROUP)
-        matrix = turn[at, :]
-        scalar = y[at, 0:C]
+        lanes, rows = tile_at(i)
+        scalar = y[rows(0), lanes]
         gating = jax.nn.sigmoid(scalar)
         slope = gating * (1.0 - gating)
-        total = jnp.zeros((GROUP, C), F32)
+        total = jnp.zeros((GROUP, LANES), F32)
         lowest = None
         for degree in range(5):
             cols = degree_cols(degree)
-            values = [xc[j // 2, at, half(j)].astype(F32) for j in cols]
+            values = [xc[rows(j), lanes].astype(F32) for j in cols]
             for k in frame_rows(degree):
                 value = None
                 for n, j in enumerate(cols):
-                    term = factor_of(matrix, k * COEF + j) * values[n]
+                    term = factor_of(k * COEF + j, lanes) * values[n]
                     value = term if value is None else value + term
                 if k == 0:
                     lowest = value
                 else:
-                    total = total + value * y[at, k * C : (k + 1) * C]
-                    grad_y[at, k * C : (k + 1) * C] = (gating * value).astype(BF16)
-        grad_y[at, 0:C] = (lowest * (gating + scalar * slope) + total * slope).astype(BF16)
+                    total = total + value * y[rows(k), lanes]
+                    grad_y[rows(k), lanes] = (gating * value).astype(BF16)
+        grad_y[rows(0), lanes] = (lowest * (gating + scalar * slope) + total * slope).astype(BF16)
         return carry
 
     lax.fori_loop(0, steps, gate, 0)
 
     def backward(i, carry):
         at = pl.ds(pl.multiple_of(i * BLOCK, BLOCK), BLOCK)
-        for begin, rows, weights in parts:
-            frame[at, 2 * begin * C : 2 * (begin + rows) * C] = dot_t(
-                grad_y[at, begin * C : (begin + rows) * C], weights[...]
+        for begin, rows, weights in ((0, 5, w0_in), (5, 8, full1), (13, 6, full2)):
+            frame[2 * begin * C : 2 * (begin + rows) * C, at] = dot(
+                weights[...], grad_y[begin * C : (begin + rows) * C, at]
             ).astype(BF16)
         return carry
 
     lax.fori_loop(0, E // BLOCK, backward, 0)
 
     def unrotate(i, carry):
-        at = pl.ds(pl.multiple_of(i * GROUP, GROUP), GROUP)
-        matrix = turn[at, :]
+        lanes, rows = tile_at(i)
         for degree in range(5):
-            rows = frame_rows(degree)
-            of_src = [frame[at, 2 * k * C : (2 * k + 1) * C].astype(F32) for k in rows]
-            of_tgt = [frame[at, (2 * k + 1) * C : (2 * k + 2) * C].astype(F32) for k in rows]
+            ks = frame_rows(degree)
+            of_src = [frame[rows(2 * k), lanes].astype(F32) for k in ks]
+            of_tgt = [frame[rows(2 * k + 1), lanes].astype(F32) for k in ks]
             for j in degree_cols(degree):
                 sums = [None, None]
-                for n, k in enumerate(rows):
-                    factor = factor_of(matrix, k * COEF + j)
+                for n, k in enumerate(ks):
+                    factor = factor_of(k * COEF + j, lanes)
                     for which, values in enumerate((of_src, of_tgt)):
                         term = factor * values[n]
                         sums[which] = term if sums[which] is None else sums[which] + term
-                xs[j // 2, at, half(j)] = sums[0].astype(BF16)
-                xf[j // 2, at, half(j)] = sums[1].astype(BF16)
+                xs[rows(j), lanes] = sums[0].astype(BF16)
+                xf[rows(j), lanes] = sums[1].astype(BF16)
         return carry
 
     lax.fori_loop(0, steps, unrotate, 0)
 
     def scatter(marks, grads, to, lead):
         for p in range(PAIRS):
-            both = dot(marks[...], grads[p])
+            both = dot_t(marks[...], grads[2 * p * C : 2 * (p + 1) * C, :])
             for j in (2 * p, 2 * p + 1):
                 if j < COEF:
-                    value = both[:, half(j)].reshape(lead + (A, C)).astype(BF16)
+                    value = both[:, (j % 2) * C : (j % 2 + 1) * C]
+                    value = value.reshape(lead + (A, C)).astype(BF16)
                     if len(lead) == 3:
                         to[:, :, :, j] = value
                     else:
                         to[:, :, j] = value
 
-    scatter(back_s, xs, src_sum, (4, 2))
+    scatter(mark_s, xs, src_sum, (4, 2))
     sib = net.push(src_sum.at[:, 1 - net.core], reduce_scratch[2], net.peer(core=1))
-    scatter(back_t, xf, tgt_sum, (4, 2, 4))
+    scatter(mark_t, xf, tgt_sum, (4, 2, 4))
     reduce_body(net, sib, tgt_sum, src_sum, out, reduce_scratch)
     for copy in net.copies:
         copy.wait_send()
@@ -528,17 +553,18 @@
         pltpu.VMEM(w0.shape, BF16),
         pltpu.VMEM((2 * w1.shape[1], 2 * w1.shape[2]), BF16),
         pltpu.VMEM((2 * w2.shape[1], 2 * w2.shape[2]), BF16),
-        pltpu.VMEM((E, FRAME * COEF), F32),
-        pltpu.VMEM((E, TGT), BF16),
-        pltpu.VMEM((E, SRC), BF16),
+        pltpu.VMEM(w0.shape[::-1], BF16),
+        pltpu.VMEM((2 * w1.shape[2], 2 * w1.shape[1]), BF16),
+        pltpu.VMEM((2 * w2.shape[2], 2 * w2.shape[1]), BF16),
+        pltpu.VMEM((FRAME * COEF, E), F32),
         pltpu.VMEM((TGT, E), BF16),
         pltpu.VMEM((SRC, E), BF16),
-        pltpu.VMEM((PAIRS, E, 2 * C), BF16),
-        pltpu.VMEM((PAIRS, E, 2 * C), BF16),
-        pltpu.VMEM((PAIRS, E, 2 * C), BF16),
-        pltpu.VMEM((E, FRAME * 2 * C), BF16),
-        pltpu.VMEM((E, FRAME * C), BF16),
-        pltpu.VMEM((E, FRAME * C), F32),
+        pltpu.VMEM((PAIRS * 2 * C, E), BF16),
+        pltpu.VMEM((PAIRS * 2 * C, E), BF16),
+        pltpu.VMEM((PAIRS * 2 * C, E), BF16),
+        pltpu.VMEM((FRAME * 2 * C, E), BF16),
+        pltpu.VMEM((FRAME * C, E), BF16),
+        pltpu.VMEM((FRAME * C, E), F32),
         buffer(4, 2, 4, COEF),
         buffer(4, 2, COEF),
         pltpu.SemaphoreType.DMA((12,)),

time: 118 us -> 91 us (0.77); the launches traced: 118 us -> 89.5 us
  Pallas kernels: 116 us -> 87.3 us
    pallas_call x1, Pallas kernels: 116 us -> 87.3 us  [fused(): pl.pallas_call(fused_kernel, out_shape=jax.ShapeDtypeStruct((COEF, A, C),...]
where the time goes in v4:
time: 91 us; the launch traced here: 89.5 us
  Pallas kernels  87.3 us (96%)
  local copies, waits for them, and re-layouts  1.54 us (2%)
    pallas_call x1, Pallas kernels, fused(): pl.pallas_call(fused_kernel, out_shape=jax.ShapeDtypeStruct((COEF, A, C),...  87.3 us

profile of v4, /device:TPU:2, one launch (start us, length us, event | category | flops | bytes accessed | tf_op | source)
XLA Modules:
  0.0 89.5 jit_solution(5909789312527159796)
XLA Ops:
  0.7 87.3 %edge_gradients.1 = f32[25,8,128]{2,1,0:T(8,128)} custom-call(s32[1,1]{1,0:T(1,128)S(6)} %copy.11.count, s32[1,512]{1,0:T(1,128)} %bitcast.12, s32[1,512]{1,0:T(1,128)} %bitcast.13, bf16[475,512]{1,0:T(8,128)(2,1)} %bitcast.8, bf16[25,8,128]{2,1,0:T(8,128)(2,1)} %bitcast.10, bf16[25,8,128]{2,1,0:T(8,128)(2,1)} %bitcast.11, bf16[1280,640]{1,0:T(8,128)(2,1)} %w0.1, ...), custom_call_target="tpu_custom_call" | custom-call | tf_op jit(solution)/shard_map/edge_gradients/pallas_call | solution.py:599
  88.0 1.5 %copy.12 = f32[8,25,128]{2,0,1:T(8,128)} copy(f32[8,25,128]{2,0,1:T(8,128)} %bitcast.9) | data formatting | bytes 204800

commit v5 on v4

--- a/solution.py
+++ b/solution.py
@@ -38,35 +38,35 @@
     return list(range(degree * degree, (degree + 1) * (degree + 1)))
 
 
-def ring(value, step):
-    return lax.rem(value + step, 4)
-
-
 class Net:
     def __init__(self, send, recv):
         row = lax.axis_index("row")
         col = lax.axis_index("col")
-        self.x = lax.div(col, 8)
-        self.z = lax.rem(lax.div(col, 4), 2)
-        self.y = lax.rem(col, 4)
-        self.high = lax.div(row, 2)
-        self.core = lax.rem(row, 2)
+        self.x = x = lax.div(col, 8)
+        self.z = z = lax.rem(lax.div(col, 4), 2)
+        self.y = y = lax.rem(col, 4)
+        self.high = high = lax.div(row, 2)
+        self.core = core = lax.rem(row, 2)
+        self.along_x = {
+            step: (row, lax.rem(x + step, 4) * 8 + z * 4 + y) for step in (1, 3)
+        }
+        self.along_y = {
+            step: (row, x * 8 + z * 4 + lax.rem(y + step, 4)) for step in (1, 3)
+        }
+        self.along_z = (row, x * 8 + (1 - z) * 4 + y)
+        self.along_high = {
+            step: (lax.rem(high + step, 4) * 2 + core, col) for step in (1, 2, 3)
+        }
+        self.sibling = (high * 2 + 1 - core, col)
         self.send = send
         self.recv = recv
         self.copies = []
-
-    def at(self, x=0, z=0, y=0):
-        z_now = 1 - self.z if z else self.z
-        return {"col": ring(self.x, x) * 8 + z_now * 4 + ring(self.y, y)}
-
-    def peer(self, high=0, core=0):
-        core_now = 1 - self.core if core else self.core
-        return {"row": ring(self.high, high) * 2 + core_now}
+        self.sent = 0
 
     def greet(self):
         barrier = pltpu.get_barrier_semaphore()
-        devices = [self.at(x=1), self.at(x=3), self.at(y=1), self.at(y=3), self.at(z=1)]
-        devices += [self.peer(high=step) for step in (1, 2, 3)] + [self.peer(core=1)]
+        devices = list(self.along_x.values()) + list(self.along_y.values()) + [self.along_z]
+        devices += list(self.along_high.values()) + [self.sibling]
         for device in devices:
             pl.semaphore_signal(barrier, inc=1, device_id=device, device_id_type=MESH)
         pl.semaphore_wait(barrier, len(devices))
@@ -85,6 +85,11 @@
         self.copies.append(copy)
         return copy
 
+    def settle(self, count):
+        for copy in self.copies[self.sent : count]:
+            copy.wait_send()
+        self.sent = count
+
 
 QUARTERS = ((0, 7), (7, 13), (13, 19), (19, 25))
 HALVES = ((0, 13), (13, 25))
@@ -102,16 +107,17 @@
 def reduce_body(net, sib, tgt, src, out, scratch):
     row_in, row_sum, sib_in, z_in, z_out, kept = scratch[:6]
     halves = (scratch[6:18], scratch[18:30])
+    before = len(net.copies) - 1
 
     def toward(h, phase, sign):
         along_x = (h == 0) == (phase == 0)
-        return net.at(x=sign) if along_x else net.at(y=sign)
+        return (net.along_x if along_x else net.along_y)[sign]
 
     def block(h, step, piece):
         bounds = QUARTERS[2 * h + piece]
         if h == 0:
-            return tgt.at[ring(net.x, step), :, :, span(bounds)]
-        return tgt.at[:, :, ring(net.y, step), span(bounds)]
+            return tgt.at[step, :, :, span(bounds)]
+        return tgt.at[:, :, step, span(bounds)]
 
     def tail(h, piece):
         first = QUARTERS[2 * h][0]
@@ -131,11 +137,11 @@
 
     sib.wait_recv()
     for high in range(4):
-        row_sum[high] = (src[high, net.core].astype(F32) + sib_in[high].astype(F32)).astype(BF16)
+        row_sum[high] = (src[high, 0].astype(F32) + sib_in[high].astype(F32)).astype(BF16)
     rows = [
-        net.push(row_sum.at[ring(net.high, step)], row_in.at[net.high], net.peer(high=step))
-        for step in (2, 1, 3)
+        net.push(row_sum.at[step], row_in.at[4 - step], net.along_high[step]) for step in (2, 1, 3)
     ]
+    net.settle(before)
 
     joined = {}
     for sign, piece in ((1, 0), (3, 1)):
@@ -157,139 +163,151 @@
         for sign in (1, 3):
             direct[h, sign].wait_recv()
             joined[h, sign].wait_recv()
-        for i in range(end_p.shape[0]):
-            for j in range(end_p.shape[1]):
+
+        def add(first):
+            for i in range(2):
                 if h == 0:
-                    mine, to = tgt[net.x, i, j, 0:13], total.at[j, i]
+                    mine, one, two = tgt[0, i, first, 0:13], end_p[i, first], end_m[i, first]
                 else:
-                    mine, to = tgt[i, j, net.y, 13:25], total.at[i, j]
-                to[...] = (
-                    mine.astype(F32) + end_p[i, j].astype(F32) + end_m[i, j].astype(F32)
+                    mine, one, two = tgt[first, i, 0, 13:25], end_p[first, i], end_m[first, i]
+                total[first, i] = (
+                    mine.astype(F32) + one.astype(F32) + two.astype(F32)
                 ).astype(BF16)
-        here = net.y if h == 0 else net.x
-        passing_2[h, 1] = net.push(
-            total.at[ring(here, 2), :, tail(h, 0)], in2_p, toward(h, 1, 1)
+
+        add(2)
+        passing_2[h, 1] = net.push(total.at[2, :, tail(h, 0)], in2_p, toward(h, 1, 1))
+        passing_2[h, 3] = net.push(total.at[2, :, tail(h, 1)], in2_m, toward(h, 1, 3))
+        add(1)
+        direct_2[h, 1] = net.push(
+            total.at[1, :, tail(h, 1)], ends.at[0, :, tail(h, 1)], toward(h, 1, 1)
         )
-        passing_2[h, 3] = net.push(
-            total.at[ring(here, 2), :, tail(h, 1)], in2_m, toward(h, 1, 3)
+        add(3)
+        direct_2[h, 3] = net.push(
+            total.at[3, :, tail(h, 0)], ends.at[1, :, tail(h, 0)], toward(h, 1, 3)
         )
-        direct_2[h, 1] = net.push(
-            total.at[ring(here, 1), :, tail(h, 1)], ends.at[0, :, tail(h, 1)], toward(h, 1, 1)
-        )
-        direct_2[h, 3] = net.push(
-            total.at[ring(here, 3), :, tail(h, 0)], ends.at[1, :, tail(h, 0)], toward(h, 1, 3)
-        )
+        add(0)
     joined_2 = {}
     for h in (0, 1):
         total, in2_p, in2_m, up2, um2, ends = halves[h][6:12]
-        here = net.y if h == 0 else net.x
         for n, (sign, piece, came, sums) in enumerate(((1, 0, in2_p, up2), (3, 1, in2_m, um2))):
             passing_2[h, sign].wait_recv()
             for i in range(2):
-                mine = total[ring(here, sign), i, tail(h, piece)]
+                mine = total[sign, i, tail(h, piece)]
                 sums[i] = (came[i].astype(F32) + mine.astype(F32)).astype(BF16)
             joined_2[h, sign] = net.push(sums, ends.at[n, :, tail(h, piece)], toward(h, 1, sign))
     for copy in rows:
         copy.wait_recv()
+    value = row_sum[0].astype(F32)
+    for step in (1, 2, 3):
+        value = value + row_in[step].astype(F32)
+    kept[...] = value
     across = []
     for h in (0, 1):
         total, in2_p, in2_m, up2, um2, ends = halves[h][6:12]
-        here = net.y if h == 0 else net.x
         for sign in (1, 3):
             direct_2[h, sign].wait_recv()
             joined_2[h, sign].wait_recv()
         at = span(HALVES[h])
-        for z_now, to in ((1 - net.z, z_out), (net.z, kept)):
-            value = total[here, z_now].astype(F32) + ends[0, z_now].astype(F32)
-            value = value + ends[1, z_now].astype(F32)
-            to[at] = value.astype(to.dtype)
-        across.append(net.push(z_out.at[at], z_in.at[at], net.at(z=1)))
-    value = kept[...] + row_sum[net.high].astype(F32)
-    for step in (1, 2, 3):
-        value = value + row_in[ring(net.high, step)].astype(F32)
-    kept[...] = value
+        value = total[0, 1].astype(F32) + ends[0, 1].astype(F32) + ends[1, 1].astype(F32)
+        z_out[at] = value.astype(BF16)
+        across.append(net.push(z_out.at[at], z_in.at[at], net.along_z))
+        value = total[0, 0].astype(F32) + ends[0, 0].astype(F32) + ends[1, 0].astype(F32)
+        kept[at] = kept[at] + value
+    net.settle(len(net.copies))
     for copy in across:
         copy.wait_recv()
     out[...] = kept[...] + z_in[...].astype(F32)
 
 
 class Flow:
-    def __init__(self, net, own, full):
+    def __init__(self, net, own, full, early):
         self.net = net
         self.own = own
         self.full = full
-        self.inner = {}
-        self.outer = {}
+        self.early = early
+        self.arrivals = {}
         self.passed = {}
         self.last = []
 
     def place(self, h, outer, inner, z, bounds):
-        net = self.net
-        near, far = (inner, outer) if h == 0 else (outer, inner)
-        z_now = (net.z, 1 - net.z, slice(0, 2))[z]
-        return self.full.at[ring(net.x, far), z_now, ring(net.y, near), span(bounds)]
+        z_now = slice(0, 2) if z == 2 else z
+        x, y = (outer, inner) if h == 0 else (inner, outer)
+        return self.full.at[x, z_now, y, span(bounds)]
 
     def step_to(self, h, phase, sign):
         along_y = (h == 0) == (phase == 0)
-        return self.net.at(y=sign) if along_y else self.net.at(x=sign)
+        return (self.net.along_y if along_y else self.net.along_x)[sign]
+
+    def inward(self, h, z):
+        source = self.place(h, 0, 0, z, HALVES[h])
+        if z == 0:
+            source = self.own.at[span(HALVES[h])]
+        for sign in (1, 3):
+            target = self.place(h, 0, 4 - sign, z, HALVES[h])
+            copy = self.net.push(source, target, self.step_to(h, 0, sign))
+            self.arrivals.setdefault((h, "inner", sign), []).append(copy)
 
     def spread(self, h, inner, z):
-        block = self.place(h, 0, inner, z, HALVES[h])
-        source = self.own.at[span(HALVES[h])] if (inner, z) == (0, 0) else block
+        source = self.place(h, 0, inner, z, HALVES[h])
+        if (inner, z) == (0, 0):
+            source = self.own.at[span(HALVES[h])]
         for sign in (1, 3):
-            self.outer[h, z, inner, sign] = self.net.push(source, block, self.step_to(h, 1, sign))
-
-    def relay(self, h, z, inner):
+            target = self.place(h, 4 - sign, inner, z, HALVES[h])
+            copy = self.net.push(source, target, self.step_to(h, 1, sign))
+            self.arrivals.setdefault((h, inner, sign), []).append(copy)
+
+    def arrive(self, *key):
+        for copy in self.arrivals[key]:
+            copy.wait_recv()
+
+    def relay(self, inner):
         for sign, quarter in ((1, 0), (3, 1)):
-            self.outer[h, z, inner, sign].wait_recv()
-            block = self.place(h, 4 - sign, inner, z, QUARTERS[2 * h + quarter])
-            self.last.append(self.net.push(block, block, self.step_to(h, 1, sign)))
+            for h in (0, 1):
+                self.arrive(h, inner, sign)
+                bounds = QUARTERS[2 * h + quarter]
+                copy = self.net.push(
+                    self.place(h, 4 - sign, inner, 2, bounds),
+                    self.place(h, 2, inner, 2, bounds),
+                    self.step_to(h, 1, sign),
+                )
+                self.last.append(copy)
 
     def send_own(self):
         net = self.net
-        self.across = net.push(self.own, self.full.at[net.x, net.z, net.y], net.at(z=1))
-        for h in (0, 1):
-            for sign in (1, 3):
-                self.inner[h, 0, sign] = net.push(
-                    self.own.at[span(HALVES[h])],
-                    self.place(h, 0, 0, 0, HALVES[h]),
-                    self.step_to(h, 0, sign),
-                )
-        for h in (0, 1):
-            self.spread(h, 0, 0)
+        self.across = net.push(self.own, self.full.at[0, 1, 0], net.along_z)
+        if self.early:
+            for h in (0, 1):
+                self.inward(h, 0)
+            for h in (0, 1):
+                self.spread(h, 0, 0)
 
     def send_partner(self):
         self.across.wait_recv()
+        which = 1 if self.early else 2
         for h in (0, 1):
-            block = self.place(h, 0, 0, 1, HALVES[h])
-            for sign in (1, 3):
-                self.inner[h, 1, sign] = self.net.push(block, block, self.step_to(h, 0, sign))
+            self.inward(h, which)
         for h in (0, 1):
-            self.spread(h, 0, 1)
+            self.spread(h, 0, which)
 
     def pass_on(self):
         for sign, quarter in ((1, 0), (3, 1)):
             for h in (0, 1):
-                self.inner[h, 0, sign].wait_recv()
-                self.inner[h, 1, sign].wait_recv()
-                block = self.place(h, 0, 4 - sign, 2, QUARTERS[2 * h + quarter])
-                self.passed[h, sign] = self.net.push(block, block, self.step_to(h, 0, sign))
-                self.spread(h, 4 - sign, 2)
-
-    def relay_first(self):
-        for z in (0, 1):
+                self.arrive(h, "inner", sign)
+                bounds = QUARTERS[2 * h + quarter]
+                self.passed[h, sign] = self.net.push(
+                    self.place(h, 0, 4 - sign, 2, bounds),
+                    self.place(h, 0, 2, 2, bounds),
+                    self.step_to(h, 0, sign),
+                )
+        for inner in (3, 1):
             for h in (0, 1):
-                self.relay(h, z, 0)
+                self.spread(h, inner, 2)
 
     def spread_far(self):
         for h in (0, 1):
             self.passed[h, 1].wait_recv()
             self.passed[h, 3].wait_recv()
             self.spread(h, 2, 2)
-
-    def relay_rest(self, inner):
-        for h in (0, 1):
-            self.relay(h, 2, inner)
 
     def finish(self):
         for copy in self.last:
@@ -345,35 +363,54 @@
                     )
                 )
     mine = [
-        pltpu.make_async_copy(feats, gf.at[net.x, net.z, net.y], local_sem.at[9]),
-        pltpu.make_async_copy(cots, gc.at[net.x, net.z, net.y], local_sem.at[10]),
-        pltpu.make_async_copy(feats, gs.at[net.high, net.core], local_sem.at[11]),
+        pltpu.make_async_copy(feats, gf.at[0, 0, 0], local_sem.at[9]),
+        pltpu.make_async_copy(cots, gc.at[0, 0, 0], local_sem.at[10]),
+        pltpu.make_async_copy(feats, gs.at[0, 0], local_sem.at[11]),
     ]
     for copy in mine + loads:
         copy.start()
     net.greet()
 
-    first = Flow(net, feats, gf)
-    second = Flow(net, cots, gc)
+    first = Flow(net, feats, gf, True)
+    second = Flow(net, cots, gc, False)
     first.send_own()
-    sibling = [net.push(feats, gs.at[net.high, net.core], net.peer(core=1))]
-    rows = [net.push(feats, gs.at[net.high, net.core], net.peer(high=step)) for step in (1, 3, 2)]
+    sibling = [net.push(feats, gs.at[0, 1], net.sibling)]
+    rows = [net.push(feats, gs.at[4 - step, 0], net.along_high[step]) for step in (1, 3, 2)]
+    second.send_own()
+    for copy in mine:
+        copy.wait()
 
     valid = lax.broadcasted_iota(jnp.int32, (1, E), 1) < count[0, 0]
-    mark_t[...] = hot(jnp.where(valid, tgt_ids[...], -1), (TGT, E))
-    mark_s[...] = hot(jnp.where(valid, src_ids[...], -1), (SRC, E))
+    ids = tgt_ids[...]
+    near_x = ((ids >> 6) - net.x) & 3
+    near_z = ((ids >> 5) & 1) ^ net.z
+    near_y = ((ids >> 3) - net.y) & 3
+    ids = near_x * 64 + near_z * 32 + near_y * 8 + (ids & 7)
+    mark_t[...] = hot(jnp.where(valid, ids, -1), (TGT, E))
+    ids = src_ids[...]
+    near_high = ((ids >> 4) - net.high) & 3
+    near_core = ((ids >> 3) & 1) ^ net.core
+    ids = near_high * 16 + near_core * 8 + (ids & 7)
+    mark_s[...] = hot(jnp.where(valid, ids, -1), (SRC, E))
     first.send_partner()
     rot_wide[...] = rot[...].astype(F32)
-    for copy in mine + loads:
+    first.pass_on()
+    second.send_partner()
+    for step, copy in zip((1, 3, 2), rows):
+        copy.wait_recv()
+        sibling.append(net.push(gs.at[4 - step, 0], gs.at[4 - step, 1], net.sibling))
+    first.relay(0)
+    first.spread_far()
+    for copy in loads:
         copy.wait()
 
     def flip_zero(r, carry):
         at = pl.ds(pl.multiple_of(r * BLOCK, BLOCK), BLOCK)
-        w0_flip[:, at] = flip(w0_in[at, :])
+        value = flip(w0_in[at, :])
+        for part in range(2):
+            to = pl.ds(pl.multiple_of(part * (w0.shape[0] // 2) + r * C, C), C)
+            w0_flip[:, to] = value[:, part * C : (part + 1) * C]
         return carry
-
-    lax.fori_loop(0, w0.shape[0] // BLOCK, flip_zero, 0)
-    first.pass_on()
 
     def flip_order(weights, full, full_flip):
         k, m = weights.shape[1:]
@@ -384,87 +421,86 @@
             full[below, 0:m] = -full[below, 0:m]
             for j in range(2):
                 value = flip(full[at, j * m : (j + 1) * m])
-                full_flip[j * m : (j + 1) * m, at] = value
-                full_flip[(1 - j) * m : (2 - j) * m, below] = -value if j else value
+                for part in range(2):
+                    piece = value[:, part * C : (part + 1) * C]
+                    to = pl.ds(pl.multiple_of(part * k + r * C, C), C)
+                    full_flip[j * m : (j + 1) * m, to] = piece
+                    to = pl.ds(pl.multiple_of(part * k + k // 2 + r * C, C), C)
+                    full_flip[(1 - j) * m : (2 - j) * m, to] = -piece if j else piece
             return carry
 
         lax.fori_loop(0, k // BLOCK, body, 0)
 
-    flip_order(w1, full1, flip1)
-    first.relay_first()
-    first.spread_far()
-    for step, copy in zip((1, 3, 2), rows):
-        copy.wait_recv()
-        block = gs.at[ring(net.high, 4 - step), net.core]
-        sibling.append(net.push(block, block, net.peer(core=1)))
-    second.send_own()
-    first.relay_rest(3)
-    first.relay_rest(1)
-    flip_order(w2, full2, flip2)
-    first.relay_rest(2)
-    second.send_partner()
+    def gather_some(marks, full, rows, to):
+        for p in range(PAIRS):
+            both = []
+            for j in (2 * p, min(2 * p + 1, COEF - 1)):
+                piece = full[:, :, :, j] if len(full.shape) == 6 else full[:, :, j]
+                both.append(piece.astype(F32).reshape(rows, C))
+            block = jnp.concatenate(both, axis=1).astype(BF16)
+            to[2 * p * C : 2 * (p + 1) * C, :] = t_dot(block, marks[...]).astype(BF16)
+
+    def factor_of(entry, lanes):
+        return jnp.broadcast_to(rot_wide[entry : entry + 1, lanes], (GROUP, LANES))
+
+    def rotate_from(source, base):
+        def rotate(i, carry):
+            lanes, rows = tile_at(i)
+            for degree in range(5):
+                cols = degree_cols(degree)
+                values = [source[rows(j), lanes].astype(F32) for j in cols]
+                for k in frame_rows(degree):
+                    value = None
+                    for n, j in enumerate(cols):
+                        term = factor_of(k * COEF + j, lanes) * values[n]
+                        value = term if value is None else value + term
+                    frame[rows(base + k), lanes] = value.astype(BF16)
+            return carry
+
+        return rotate
+
+    steps = (E // LANES) * (C // GROUP)
+    parts = ((0, 5, w0_in, w0_flip), (5, 8, full1, flip1), (13, 6, full2, flip2))
+
+    def forward_from(side):
+        def forward(i, carry):
+            at = pl.ds(pl.multiple_of(i * BLOCK, BLOCK), BLOCK)
+            for begin, rows, plain, turned in parts:
+                into = slice(begin * C, (begin + rows) * C)
+                base = side * FRAME * C
+                value = dot(
+                    turned[:, side * rows * C : (side + 1) * rows * C],
+                    frame[base + begin * C : base + (begin + rows) * C, at],
+                )
+                y[into, at] = y[into, at] + value if side else value
+            return carry
+
+        return forward
+
+    rotate_src, rotate_tgt = rotate_from(xs, 0), rotate_from(xf, FRAME)
+    forward_src, forward_tgt = forward_from(0), forward_from(1)
+
+    lax.fori_loop(0, w0.shape[0] // BLOCK, flip_zero, 0)
+    first.relay(3)
+    second.pass_on()
+    first.relay(1)
     for copy in sibling:
         copy.wait_recv()
-
-    def pair_of(full, p, rows):
-        both = []
-        for j in (2 * p, jnp.minimum(2 * p + 1, COEF - 1)):
-            piece = full[:, :, :, j] if len(full.shape) == 6 else full[:, :, j]
-            both.append(piece.astype(F32).reshape(rows, C))
-        return jnp.concatenate(both, axis=1).astype(BF16)
-
-    def gather_some(marks, full, rows, to):
-        def body(p, carry):
-            at = pl.ds(pl.multiple_of(p * 2 * C, 2 * C), 2 * C)
-            to[at, :] = t_dot(pair_of(full, p, rows), marks[...]).astype(BF16)
-            return carry
-
-        lax.fori_loop(0, PAIRS, body, 0)
-
     gather_some(mark_s, gs, SRC, xs)
-    second.pass_on()
+    first.relay(2)
+    second.relay(0)
+    second.spread_far()
+    flip_order(w1, full1, flip1)
+    second.relay(3)
+    second.relay(1)
+    lax.fori_loop(0, steps, rotate_src, 0)
+    second.relay(2)
+    flip_order(w2, full2, flip2)
+    lax.fori_loop(0, E // BLOCK, forward_src, 0)
     first.finish()
-    second.relay_first()
     gather_some(mark_t, gf, TGT, xf)
-    second.spread_far()
-
-    def factor_of(entry, lanes):
-        return jnp.broadcast_to(rot_wide[entry : entry + 1, lanes], (GROUP, LANES))
-
-    def rotate(i, carry):
-        lanes, rows = tile_at(i)
-        for degree in range(5):
-            cols = degree_cols(degree)
-            from_src = [xs[rows(j), lanes].astype(F32) for j in cols]
-            from_tgt = [xf[rows(j), lanes].astype(F32) for j in cols]
-            for k in frame_rows(degree):
-                sums = [None, None]
-                for n, j in enumerate(cols):
-                    factor = factor_of(k * COEF + j, lanes)
-                    for which, values in enumerate((from_src, from_tgt)):
-                        term = factor * values[n]
-                        sums[which] = term if sums[which] is None else sums[which] + term
-                frame[rows(2 * k), lanes] = sums[0].astype(BF16)
-                frame[rows(2 * k + 1), lanes] = sums[1].astype(BF16)
-        return carry
-
-    steps = (E // LANES) * (C // GROUP)
-    lax.fori_loop(0, steps // 4, rotate, 0)
-    second.relay_rest(3)
-    second.relay_rest(1)
-    lax.fori_loop(steps // 4, steps // 2, rotate, 0)
-    second.relay_rest(2)
-    lax.fori_loop(steps // 2, steps, rotate, 0)
-
-    def forward(i, carry):
-        at = pl.ds(pl.multiple_of(i * BLOCK, BLOCK), BLOCK)
-        for begin, rows, weights in ((0, 5, w0_flip), (5, 8, flip1), (13, 6, flip2)):
-            y[begin * C : (begin + rows) * C, at] = dot(
-                weights[...], frame[2 * begin * C : 2 * (begin + rows) * C, at]
-            )
-        return carry
-
-    lax.fori_loop(0, E // BLOCK, forward, 0)
+    lax.fori_loop(0, steps, rotate_tgt, 0)
+    lax.fori_loop(0, E // BLOCK, forward_tgt, 0)
     second.finish()
     gather_some(mark_t, gc, TGT, xc)
 
@@ -495,7 +531,7 @@
 
     def backward(i, carry):
         at = pl.ds(pl.multiple_of(i * BLOCK, BLOCK), BLOCK)
-        for begin, rows, weights in ((0, 5, w0_in), (5, 8, full1), (13, 6, full2)):
+        for begin, rows, weights, turned in parts:
             frame[2 * begin * C : 2 * (begin + rows) * C, at] = dot(
                 weights[...], grad_y[begin * C : (begin + rows) * C, at]
             ).astype(BF16)
@@ -535,11 +571,9 @@
                         to[:, :, j] = value
 
     scatter(mark_s, xs, src_sum, (4, 2))
-    sib = net.push(src_sum.at[:, 1 - net.core], reduce_scratch[2], net.peer(core=1))
+    sib = net.push(src_sum.at[:, 1], reduce_scratch[2], net.sibling)
     scatter(mark_t, xf, tgt_sum, (4, 2, 4))
     reduce_body(net, sib, tgt_sum, src_sum, out, reduce_scratch)
-    for copy in net.copies:
-        copy.wait_send()
 
 
 def fused(count, src_ids, tgt_ids, rot, feats, cots, w0, w1, w2):

time: 91 us -> 83.9 us (0.922); the launches traced: 89.5 us -> 83.7 us
  Pallas kernels: 87.3 us -> 81.5 us
    pallas_call x1, Pallas kernels: 87.3 us -> 81.5 us  [fused(): pl.pallas_call(fused_kernel, out_shape=jax.ShapeDtypeStruct((COEF, A, C),...]
where the time goes in v5:
time: 83.9 us; the launch traced here: 83.7 us
  Pallas kernels  81.5 us (97%)
  local copies, waits for them, and re-layouts  1.54 us (2%)
    pallas_call x1, Pallas kernels, fused(): pl.pallas_call(fused_kernel, out_shape=jax.ShapeDtypeStruct((COEF, A, C),...  81.5 us

profile of v5, /device:TPU:2, one launch (start us, length us, event | category | flops | bytes accessed | tf_op | source)
XLA Modules:
  0.0 83.7 jit_solution(1875092516974438166)
XLA Ops:
  0.7 81.5 %edge_gradients.1 = f32[25,8,128]{2,1,0:T(8,128)} custom-call(s32[1,1]{1,0:T(1,128)S(6)} %copy.11.count, s32[1,512]{1,0:T(1,128)} %bitcast.12, s32[1,512]{1,0:T(1,128)} %bitcast.13, bf16[475,512]{1,0:T(8,128)(2,1)} %bitcast.8, bf16[25,8,128]{2,1,0:T(8,128)(2,1)} %bitcast.10, bf16[25,8,128]{2,1,0:T(8,128)(2,1)} %bitcast.11, bf16[1280,640]{1,0:T(8,128)(2,1)} %w0.1, ...), custom_call_target="tpu_custom_call" | custom-call | tf_op jit(solution)/shard_map/edge_gradients/pallas_call | solution.py:633
  82.1 1.5 %copy.12 = f32[8,25,128]{2,0,1:T(8,128)} copy(f32[8,25,128]{2,0,1:T(8,128)} %bitcast.9) | data formatting | bytes 204800

commit v6 on v5

--- a/solution.py
+++ b/solution.py
@@ -47,13 +47,13 @@
         self.y = y = lax.rem(col, 4)
         self.high = high = lax.div(row, 2)
         self.core = core = lax.rem(row, 2)
-        self.along_x = {
-            step: (row, lax.rem(x + step, 4) * 8 + z * 4 + y) for step in (1, 3)
-        }
-        self.along_y = {
-            step: (row, x * 8 + z * 4 + lax.rem(y + step, 4)) for step in (1, 3)
-        }
-        self.along_z = (row, x * 8 + (1 - z) * 4 + y)
+        zs = (z, 1 - z)
+        self.plane = {}
+        for far in (0, 1):
+            for step in range(4):
+                if step or far:
+                    self.plane[0, step, far] = (row, x * 8 + zs[far] * 4 + lax.rem(y + step, 4))
+                    self.plane[1, step, far] = (row, lax.rem(x + step, 4) * 8 + zs[far] * 4 + y)
         self.along_high = {
             step: (lax.rem(high + step, 4) * 2 + core, col) for step in (1, 2, 3)
         }
@@ -65,7 +65,7 @@
 
     def greet(self):
         barrier = pltpu.get_barrier_semaphore()
-        devices = list(self.along_x.values()) + list(self.along_y.values()) + [self.along_z]
+        devices = [self.plane[key] for key in self.plane if key != (1, 0, 1)]
         devices += list(self.along_high.values()) + [self.sibling]
         for device in devices:
             pl.semaphore_signal(barrier, inc=1, device_id=device, device_id_type=MESH)
@@ -105,13 +105,12 @@
 
 
 def reduce_body(net, sib, tgt, src, out, scratch):
-    row_in, row_sum, sib_in, z_in, z_out, kept = scratch[:6]
-    halves = (scratch[6:18], scratch[18:30])
+    row_in, row_sum, sib_in, kept = scratch[:4]
+    halves = (scratch[4:12], scratch[12:20])
     before = len(net.copies) - 1
 
-    def toward(h, phase, sign):
-        along_x = (h == 0) == (phase == 0)
-        return (net.along_x if along_x else net.along_y)[sign]
+    def toward(h, sign):
+        return net.plane[1 - h, sign, 0]
 
     def block(h, step, piece):
         bounds = QUARTERS[2 * h + piece]
@@ -128,12 +127,12 @@
     direct = {}
     for h in (0, 1):
         in_p, in_m, up, um, end_p, end_m = halves[h][:6]
-        passing[h, 1] = net.push(block(h, 2, 0), in_p, toward(h, 0, 1))
-        passing[h, 3] = net.push(block(h, 2, 1), in_m, toward(h, 0, 3))
+        passing[h, 1] = net.push(block(h, 2, 0), in_p, toward(h, 1))
+        passing[h, 3] = net.push(block(h, 2, 1), in_m, toward(h, 3))
     for h in (0, 1):
         in_p, in_m, up, um, end_p, end_m = halves[h][:6]
-        direct[h, 1] = net.push(block(h, 1, 1), end_p.at[:, :, tail(h, 1)], toward(h, 0, 1))
-        direct[h, 3] = net.push(block(h, 3, 0), end_m.at[:, :, tail(h, 0)], toward(h, 0, 3))
+        direct[h, 1] = net.push(block(h, 1, 1), end_p.at[:, :, tail(h, 1)], toward(h, 1))
+        direct[h, 3] = net.push(block(h, 3, 0), end_m.at[:, :, tail(h, 0)], toward(h, 3))
 
     sib.wait_recv()
     for high in range(4):
@@ -153,80 +152,59 @@
             for i in range(came.shape[0]):
                 for j in range(came.shape[1]):
                     sums[i, j] = (came[i, j].astype(F32) + mine[i, j].astype(F32)).astype(BF16)
-            joined[h, sign] = net.push(sums, end.at[:, :, tail(h, piece)], toward(h, 0, sign))
-
-    passing_2 = {}
-    direct_2 = {}
+            joined[h, sign] = net.push(sums, end.at[:, :, tail(h, piece)], toward(h, sign))
+
+    final = []
     for h in (0, 1):
-        in_p, in_m, up, um, end_p, end_m = halves[h][:6]
-        total, in2_p, in2_m, up2, um2, ends = halves[h][6:12]
+        in_p, in_m, up, um, end_p, end_m, total, ends = halves[h]
         for sign in (1, 3):
             direct[h, sign].wait_recv()
             joined[h, sign].wait_recv()
-
-        def add(first):
-            for i in range(2):
+        for step in (2, 1, 3, 0):
+            for far in (1, 0):
                 if h == 0:
-                    mine, one, two = tgt[0, i, first, 0:13], end_p[i, first], end_m[i, first]
+                    mine, one, two = tgt[0, far, step, 0:13], end_p[far, step], end_m[far, step]
                 else:
-                    mine, one, two = tgt[first, i, 0, 13:25], end_p[first, i], end_m[first, i]
-                total[first, i] = (
-                    mine.astype(F32) + one.astype(F32) + two.astype(F32)
-                ).astype(BF16)
-
-        add(2)
-        passing_2[h, 1] = net.push(total.at[2, :, tail(h, 0)], in2_p, toward(h, 1, 1))
-        passing_2[h, 3] = net.push(total.at[2, :, tail(h, 1)], in2_m, toward(h, 1, 3))
-        add(1)
-        direct_2[h, 1] = net.push(
-            total.at[1, :, tail(h, 1)], ends.at[0, :, tail(h, 1)], toward(h, 1, 1)
-        )
-        add(3)
-        direct_2[h, 3] = net.push(
-            total.at[3, :, tail(h, 0)], ends.at[1, :, tail(h, 0)], toward(h, 1, 3)
-        )
-        add(0)
-    joined_2 = {}
-    for h in (0, 1):
-        total, in2_p, in2_m, up2, um2, ends = halves[h][6:12]
-        for n, (sign, piece, came, sums) in enumerate(((1, 0, in2_p, up2), (3, 1, in2_m, um2))):
-            passing_2[h, sign].wait_recv()
-            for i in range(2):
-                mine = total[sign, i, tail(h, piece)]
-                sums[i] = (came[i].astype(F32) + mine.astype(F32)).astype(BF16)
-            joined_2[h, sign] = net.push(sums, ends.at[n, :, tail(h, piece)], toward(h, 1, sign))
+                    mine, one, two = tgt[step, far, 0, 13:25], end_p[step, far], end_m[step, far]
+                value = mine.astype(F32) + one.astype(F32) + two.astype(F32)
+                if step or far:
+                    total[step, far] = value.astype(BF16)
+                    final.append(
+                        net.push(
+                            total.at[step, far],
+                            ends.at[(4 - step) % 4, far],
+                            net.plane[h, step, far],
+                        )
+                    )
+                else:
+                    kept[span(HALVES[h])] = value
     for copy in rows:
         copy.wait_recv()
-    value = row_sum[0].astype(F32)
+    value = kept[...] + row_sum[0].astype(F32)
     for step in (1, 2, 3):
         value = value + row_in[step].astype(F32)
     kept[...] = value
-    across = []
+    net.settle(len(net.copies))
+    for copy in final:
+        copy.wait_recv()
     for h in (0, 1):
-        total, in2_p, in2_m, up2, um2, ends = halves[h][6:12]
-        for sign in (1, 3):
-            direct_2[h, sign].wait_recv()
-            joined_2[h, sign].wait_recv()
+        ends = halves[h][7]
         at = span(HALVES[h])
-        value = total[0, 1].astype(F32) + ends[0, 1].astype(F32) + ends[1, 1].astype(F32)
-        z_out[at] = value.astype(BF16)
-        across.append(net.push(z_out.at[at], z_in.at[at], net.along_z))
-        value = total[0, 0].astype(F32) + ends[0, 0].astype(F32) + ends[1, 0].astype(F32)
-        kept[at] = kept[at] + value
-    net.settle(len(net.copies))
-    for copy in across:
-        copy.wait_recv()
-    out[...] = kept[...] + z_in[...].astype(F32)
+        value = kept[at]
+        for step in range(4):
+            for far in (0, 1):
+                if step or far:
+                    value = value + ends[step, far].astype(F32)
+        out[at] = value
 
 
 class Flow:
-    def __init__(self, net, own, full, early):
+    def __init__(self, net, own, full):
         self.net = net
         self.own = own
         self.full = full
-        self.early = early
         self.arrivals = {}
-        self.passed = {}
+        self.outer = {}
         self.last = []
 
     def place(self, h, outer, inner, z, bounds):
@@ -234,80 +212,43 @@
         x, y = (outer, inner) if h == 0 else (inner, outer)
         return self.full.at[x, z_now, y, span(bounds)]
 
-    def step_to(self, h, phase, sign):
-        along_y = (h == 0) == (phase == 0)
-        return (self.net.along_y if along_y else self.net.along_x)[sign]
-
-    def inward(self, h, z):
-        source = self.place(h, 0, 0, z, HALVES[h])
-        if z == 0:
-            source = self.own.at[span(HALVES[h])]
-        for sign in (1, 3):
-            target = self.place(h, 0, 4 - sign, z, HALVES[h])
-            copy = self.net.push(source, target, self.step_to(h, 0, sign))
-            self.arrivals.setdefault((h, "inner", sign), []).append(copy)
-
-    def spread(self, h, inner, z):
-        source = self.place(h, 0, inner, z, HALVES[h])
-        if (inner, z) == (0, 0):
-            source = self.own.at[span(HALVES[h])]
-        for sign in (1, 3):
-            target = self.place(h, 4 - sign, inner, z, HALVES[h])
-            copy = self.net.push(source, target, self.step_to(h, 1, sign))
-            self.arrivals.setdefault((h, inner, sign), []).append(copy)
-
-    def arrive(self, *key):
-        for copy in self.arrivals[key]:
-            copy.wait_recv()
+    def send_own(self):
+        for step, far in ((0, 1), (1, 0), (3, 0), (1, 1), (3, 1), (2, 0), (2, 1)):
+            for h in (0, 1):
+                inner = (4 - step) % 4
+                self.arrivals[h, inner, far] = self.net.push(
+                    self.own.at[span(HALVES[h])],
+                    self.place(h, 0, inner, far, HALVES[h]),
+                    self.net.plane[h, step, far],
+                )
+            if step == 3 and not far:
+                self.spread(0, 0)
+
+    def spread(self, inner, z):
+        for h in (0, 1):
+            for far in (0, 1) if z == 2 else (z,):
+                if inner or far:
+                    self.arrivals[h, inner, far].wait_recv()
+            source = self.place(h, 0, inner, z, HALVES[h])
+            if (inner, z) == (0, 0):
+                source = self.own.at[span(HALVES[h])]
+            for sign in (1, 3):
+                target = self.place(h, 4 - sign, inner, z, HALVES[h])
+                copy = self.net.push(source, target, self.net.plane[1 - h, sign, 0])
+                self.outer.setdefault((h, inner, sign), []).append(copy)
 
     def relay(self, inner):
         for sign, quarter in ((1, 0), (3, 1)):
             for h in (0, 1):
-                self.arrive(h, inner, sign)
+                for copy in self.outer[h, inner, sign]:
+                    copy.wait_recv()
                 bounds = QUARTERS[2 * h + quarter]
                 copy = self.net.push(
                     self.place(h, 4 - sign, inner, 2, bounds),
                     self.place(h, 2, inner, 2, bounds),
-                    self.step_to(h, 1, sign),
+                    self.net.plane[1 - h, sign, 0],
                 )
                 self.last.append(copy)
-
-    def send_own(self):
-        net = self.net
-        self.across = net.push(self.own, self.full.at[0, 1, 0], net.along_z)
-        if self.early:
-            for h in (0, 1):
-                self.inward(h, 0)
-            for h in (0, 1):
-                self.spread(h, 0, 0)
-
-    def send_partner(self):
-        self.across.wait_recv()
-        which = 1 if self.early else 2
-        for h in (0, 1):
-            self.inward(h, which)
-        for h in (0, 1):
-            self.spread(h, 0, which)
-
-    def pass_on(self):
-        for sign, quarter in ((1, 0), (3, 1)):
-            for h in (0, 1):
-                self.arrive(h, "inner", sign)
-                bounds = QUARTERS[2 * h + quarter]
-                self.passed[h, sign] = self.net.push(
-                    self.place(h, 0, 4 - sign, 2, bounds),
-                    self.place(h, 0, 2, 2, bounds),
-                    self.step_to(h, 0, sign),
-                )
-        for inner in (3, 1):
-            for h in (0, 1):
-                self.spread(h, inner, 2)
-
-    def spread_far(self):
-        for h in (0, 1):
-            self.passed[h, 1].wait_recv()
-            self.passed[h, 3].wait_recv()
-            self.spread(h, 2, 2)
 
     def finish(self):
         for copy in self.last:
@@ -371,12 +312,11 @@
         copy.start()
     net.greet()
 
-    first = Flow(net, feats, gf, True)
-    second = Flow(net, cots, gc, False)
+    first = Flow(net, feats, gf)
+    second = Flow(net, cots, gc)
     first.send_own()
     sibling = [net.push(feats, gs.at[0, 1], net.sibling)]
     rows = [net.push(feats, gs.at[4 - step, 0], net.along_high[step]) for step in (1, 3, 2)]
-    second.send_own()
     for copy in mine:
         copy.wait()
 
@@ -392,15 +332,16 @@
     near_core = ((ids >> 3) & 1) ^ net.core
     ids = near_high * 16 + near_core * 8 + (ids & 7)
     mark_s[...] = hot(jnp.where(valid, ids, -1), (SRC, E))
-    first.send_partner()
+    first.spread(0, 1)
+    first.spread(3, 2)
+    first.spread(1, 2)
     rot_wide[...] = rot[...].astype(F32)
-    first.pass_on()
-    second.send_partner()
+    first.spread(2, 2)
+    second.send_own()
     for step, copy in zip((1, 3, 2), rows):
         copy.wait_recv()
         sibling.append(net.push(gs.at[4 - step, 0], gs.at[4 - step, 1], net.sibling))
     first.relay(0)
-    first.spread_far()
     for copy in loads:
         copy.wait()
 
@@ -482,14 +423,15 @@
 
     lax.fori_loop(0, w0.shape[0] // BLOCK, flip_zero, 0)
     first.relay(3)
-    second.pass_on()
     first.relay(1)
+    second.spread(0, 1)
     for copy in sibling:
         copy.wait_recv()
     gather_some(mark_s, gs, SRC, xs)
     first.relay(2)
+    for inner in (3, 1, 2):
+        second.spread(inner, 2)
     second.relay(0)
-    second.spread_far()
     flip_order(w1, full1, flip1)
     second.relay(3)
     second.relay(1)
@@ -607,8 +549,6 @@
         buffer(4, COEF),
         buffer(4, COEF),
         buffer(4, COEF),
-        buffer(COEF),
-        buffer(COEF),
         pltpu.VMEM((COEF, A, C), F32),
     ]
     for h, lead in ((0, (2, 4)), (1, (4, 2))):
@@ -622,11 +562,7 @@
             buffer(*lead, whole),
             buffer(*lead, whole),
             buffer(4, 2, whole),
-            buffer(2, plus),
-            buffer(2, minus),
-            buffer(2, plus),
-            buffer(2, minus),
-            buffer(2, 2, whole),
+            buffer(4, 2, whole),
         ]
     vmem = pl.BlockSpec(memory_space=pltpu.VMEM)
     hbm = pl.BlockSpec(memory_space=pl.ANY)

time: 83.9 us -> 79.9 us (0.952)
  Pallas kernels: 81.5 us -> 77.4 us
    pallas_call x1, Pallas kernels: 81.5 us -> 77.4 us  [fused(): pl.pallas_call(fused_kernel, out_shape=jax.ShapeDtypeStruct((COEF, A, C),...]
where the time goes in v6:
time: 79.9 us; the launch traced here: 79.6 us
  Pallas kernels  77.4 us (97%)
  local copies, waits for them, and re-layouts  1.54 us (2%)
    pallas_call x1, Pallas kernels, fused(): pl.pallas_call(fused_kernel, out_shape=jax.ShapeDtypeStruct((COEF, A, C),...  77.4 us

profile of v6, /device:TPU:2, one launch (start us, length us, event | category | flops | bytes accessed | tf_op | source)
XLA Modules:
  0.0 79.6 jit_solution(11068009563402449259)
XLA Ops:
  0.7 77.4 %edge_gradients.1 = f32[25,8,128]{2,1,0:T(8,128)} custom-call(s32[1,1]{1,0:T(1,128)S(6)} %copy.11.count, s32[1,512]{1,0:T(1,128)} %bitcast.12, s32[1,512]{1,0:T(1,128)} %bitcast.13, bf16[475,512]{1,0:T(8,128)(2,1)} %bitcast.8, bf16[25,8,128]{2,1,0:T(8,128)(2,1)} %bitcast.10, bf16[25,8,128]{2,1,0:T(8,128)(2,1)} %bitcast.11, bf16[1280,640]{1,0:T(8,128)(2,1)} %w0.1, ...), custom_call_target="tpu_custom_call" | custom-call | tf_op jit(solution)/shard_map/edge_gradients/pallas_call | solution.py:569
  78.1 1.5 %copy.12 = f32[8,25,128]{2,0,1:T(8,128)} copy(f32[8,25,128]{2,0,1:T(8,128)} %bitcast.9) | data formatting | bytes 204800

commit v7 on v6

--- a/solution.py
+++ b/solution.py
@@ -91,8 +91,8 @@
         self.sent = count
 
 
-QUARTERS = ((0, 7), (7, 13), (13, 19), (19, 25))
-HALVES = ((0, 13), (13, 25))
+QUARTERS = ((0, 6), (6, 12), (12, 18), (18, 25))
+HALVES = ((0, 12), (12, 25))
 MESSAGES = 160
 
 
@@ -104,98 +104,108 @@
     return bounds[1] - bounds[0]
 
 
-def reduce_body(net, sib, tgt, src, out, scratch):
-    row_in, row_sum, sib_in, kept = scratch[:4]
-    halves = (scratch[4:12], scratch[12:20])
-    before = len(net.copies) - 1
-
-    def toward(h, sign):
-        return net.plane[1 - h, sign, 0]
-
-    def block(h, step, piece):
+class Reduction:
+    def __init__(self, net, tgt, src, out, scratch):
+        self.net = net
+        self.tgt = tgt
+        self.src = src
+        self.out = out
+        self.row_in, self.row_sum, self.sib_in, self.kept = scratch[:4]
+        self.halves = (scratch[4:12], scratch[12:20])
+        self.passing = {}
+        self.direct = {}
+
+    def toward(self, h, sign):
+        return self.net.plane[1 - h, sign, 0]
+
+    def block(self, h, step, piece):
         bounds = QUARTERS[2 * h + piece]
         if h == 0:
-            return tgt.at[step, :, :, span(bounds)]
-        return tgt.at[:, :, step, span(bounds)]
-
-    def tail(h, piece):
+            return self.tgt.at[step, :, :, span(bounds)]
+        return self.tgt.at[:, :, step, span(bounds)]
+
+    def tail(self, h, piece):
         first = QUARTERS[2 * h][0]
         bounds = QUARTERS[2 * h + piece]
         return pl.ds(bounds[0] - first, length(bounds))
 
-    passing = {}
-    direct = {}
-    for h in (0, 1):
-        in_p, in_m, up, um, end_p, end_m = halves[h][:6]
-        passing[h, 1] = net.push(block(h, 2, 0), in_p, toward(h, 1))
-        passing[h, 3] = net.push(block(h, 2, 1), in_m, toward(h, 3))
-    for h in (0, 1):
-        in_p, in_m, up, um, end_p, end_m = halves[h][:6]
-        direct[h, 1] = net.push(block(h, 1, 1), end_p.at[:, :, tail(h, 1)], toward(h, 1))
-        direct[h, 3] = net.push(block(h, 3, 0), end_m.at[:, :, tail(h, 0)], toward(h, 3))
-
-    sib.wait_recv()
-    for high in range(4):
-        row_sum[high] = (src[high, 0].astype(F32) + sib_in[high].astype(F32)).astype(BF16)
-    rows = [
-        net.push(row_sum.at[step], row_in.at[4 - step], net.along_high[step]) for step in (2, 1, 3)
-    ]
-    net.settle(before)
-
-    joined = {}
-    for sign, piece in ((1, 0), (3, 1)):
-        for h in (0, 1):
-            in_p, in_m, up, um, end_p, end_m = halves[h][:6]
-            came, sums, end = (in_p, up, end_p) if sign == 1 else (in_m, um, end_m)
-            passing[h, sign].wait_recv()
-            mine = block(h, sign, piece)
+    def start_rows(self):
+        self.before = len(self.net.copies)
+        self.sib = self.net.push(self.src.at[:, 1], self.sib_in, self.net.sibling)
+
+    def send_rows(self):
+        self.sib.wait_recv()
+        for high in range(4):
+            value = self.src[high, 0].astype(F32) + self.sib_in[high].astype(F32)
+            self.row_sum[high] = value.astype(BF16)
+        self.rows = [
+            self.net.push(
+                self.row_sum.at[step], self.row_in.at[4 - step], self.net.along_high[step]
+            )
+            for step in (2, 1, 3)
+        ]
+
+    def start(self, h):
+        in_p, in_m, up, um, end_p, end_m = self.halves[h][:6]
+        push, block, tail, toward = self.net.push, self.block, self.tail, self.toward
+        self.passing[h, 1] = push(block(h, 2, 0), in_p, toward(h, 1))
+        self.passing[h, 3] = push(block(h, 2, 1), in_m, toward(h, 3))
+        self.direct[h, 1] = push(block(h, 1, 1), end_p.at[:, :, tail(h, 1)], toward(h, 1))
+        self.direct[h, 3] = push(block(h, 3, 0), end_m.at[:, :, tail(h, 0)], toward(h, 3))
+
+    def join(self, h):
+        in_p, in_m, up, um, end_p, end_m = self.halves[h][:6]
+        for sign, piece, came, sums, end in ((1, 0, in_p, up, end_p), (3, 1, in_m, um, end_m)):
+            self.passing[h, sign].wait_recv()
+            mine = self.block(h, sign, piece)
             for i in range(came.shape[0]):
                 for j in range(came.shape[1]):
                     sums[i, j] = (came[i, j].astype(F32) + mine[i, j].astype(F32)).astype(BF16)
-            joined[h, sign] = net.push(sums, end.at[:, :, tail(h, piece)], toward(h, sign))
-
-    final = []
-    for h in (0, 1):
-        in_p, in_m, up, um, end_p, end_m, total, ends = halves[h]
+            target = end.at[:, :, self.tail(h, piece)]
+            self.passing[h, sign] = self.net.push(sums, target, self.toward(h, sign))
+
+    def spread(self, h):
+        in_p, in_m, up, um, end_p, end_m, total, ends = self.halves[h]
         for sign in (1, 3):
-            direct[h, sign].wait_recv()
-            joined[h, sign].wait_recv()
+            self.direct[h, sign].wait_recv()
+            self.passing[h, sign].wait_recv()
+        at = slice(*HALVES[h])
+        final = []
         for step in (2, 1, 3, 0):
             for far in (1, 0):
                 if h == 0:
-                    mine, one, two = tgt[0, far, step, 0:13], end_p[far, step], end_m[far, step]
+                    mine, one, two = self.tgt[0, far, step, at], end_p[far, step], end_m[far, step]
                 else:
-                    mine, one, two = tgt[step, far, 0, 13:25], end_p[step, far], end_m[step, far]
+                    mine, one, two = self.tgt[step, far, 0, at], end_p[step, far], end_m[step, far]
                 value = mine.astype(F32) + one.astype(F32) + two.astype(F32)
                 if step or far:
                     total[step, far] = value.astype(BF16)
-                    final.append(
-                        net.push(
-                            total.at[step, far],
-                            ends.at[(4 - step) % 4, far],
-                            net.plane[h, step, far],
-                        )
-                    )
+                    target = ends.at[(4 - step) % 4, far]
+                    device = self.net.plane[h, step, far]
+                    final.append(self.net.push(total.at[step, far], target, device))
                 else:
-                    kept[span(HALVES[h])] = value
-    for copy in rows:
-        copy.wait_recv()
-    value = kept[...] + row_sum[0].astype(F32)
-    for step in (1, 2, 3):
-        value = value + row_in[step].astype(F32)
-    kept[...] = value
-    net.settle(len(net.copies))
-    for copy in final:
-        copy.wait_recv()
-    for h in (0, 1):
-        ends = halves[h][7]
-        at = span(HALVES[h])
-        value = kept[at]
+                    self.kept[at] = value
+        return final
+
+    def add_rows(self):
+        for copy in self.rows:
+            copy.wait_recv()
+        value = self.kept[...] + self.row_sum[0].astype(F32)
+        for step in (1, 2, 3):
+            value = value + self.row_in[step].astype(F32)
+        self.kept[...] = value
+
+    def close(self, h, final):
+        for copy in final:
+            copy.wait_recv()
+        ends = self.halves[h][7]
+        at = slice(*HALVES[h])
+        value = self.kept[at]
         for step in range(4):
             for far in (0, 1):
                 if step or far:
                     value = value + ends[step, far].astype(F32)
-        out[at] = value
+        self.out[at] = value
 
 
 class Flow:
@@ -333,17 +343,10 @@
     ids = near_high * 16 + near_core * 8 + (ids & 7)
     mark_s[...] = hot(jnp.where(valid, ids, -1), (SRC, E))
     first.spread(0, 1)
-    first.spread(3, 2)
-    first.spread(1, 2)
     rot_wide[...] = rot[...].astype(F32)
-    first.spread(2, 2)
+    for inner in (3, 1, 2):
+        first.spread(inner, 2)
     second.send_own()
-    for step, copy in zip((1, 3, 2), rows):
-        copy.wait_recv()
-        sibling.append(net.push(gs.at[4 - step, 0], gs.at[4 - step, 1], net.sibling))
-    first.relay(0)
-    for copy in loads:
-        copy.wait()
 
     def flip_zero(r, carry):
         at = pl.ds(pl.multiple_of(r * BLOCK, BLOCK), BLOCK)
@@ -421,23 +424,29 @@
     rotate_src, rotate_tgt = rotate_from(xs, 0), rotate_from(xf, FRAME)
     forward_src, forward_tgt = forward_from(0), forward_from(1)
 
+    for copy in loads:
+        copy.wait()
     lax.fori_loop(0, w0.shape[0] // BLOCK, flip_zero, 0)
+    first.relay(0)
+    for step, copy in zip((1, 3, 2), rows):
+        copy.wait_recv()
+        sibling.append(net.push(gs.at[4 - step, 0], gs.at[4 - step, 1], net.sibling))
     first.relay(3)
     first.relay(1)
     second.spread(0, 1)
+    flip_order(w2, full2, flip2)
+    first.relay(2)
+    for inner in (3, 1, 2):
+        second.spread(inner, 2)
+    flip_order(w1, full1, flip1)
+    second.relay(0)
     for copy in sibling:
         copy.wait_recv()
     gather_some(mark_s, gs, SRC, xs)
-    first.relay(2)
-    for inner in (3, 1, 2):
-        second.spread(inner, 2)
-    second.relay(0)
-    flip_order(w1, full1, flip1)
     second.relay(3)
     second.relay(1)
     lax.fori_loop(0, steps, rotate_src, 0)
     second.relay(2)
-    flip_order(w2, full2, flip2)
     lax.fori_loop(0, E // BLOCK, forward_src, 0)
     first.finish()
     gather_some(mark_t, gf, TGT, xf)
@@ -481,27 +490,27 @@
 
     lax.fori_loop(0, E // BLOCK, backward, 0)
 
-    def unrotate(i, carry):
-        lanes, rows = tile_at(i)
-        for degree in range(5):
-            ks = frame_rows(degree)
-            of_src = [frame[rows(2 * k), lanes].astype(F32) for k in ks]
-            of_tgt = [frame[rows(2 * k + 1), lanes].astype(F32) for k in ks]
-            for j in degree_cols(degree):
-                sums = [None, None]
-                for n, k in enumerate(ks):
-                    factor = factor_of(k * COEF + j, lanes)
-                    for which, values in enumerate((of_src, of_tgt)):
-                        term = factor * values[n]
-                        sums[which] = term if sums[which] is None else sums[which] + term
-                xs[rows(j), lanes] = sums[0].astype(BF16)
-                xf[rows(j), lanes] = sums[1].astype(BF16)
-        return carry
-
-    lax.fori_loop(0, steps, unrotate, 0)
-
-    def scatter(marks, grads, to, lead):
-        for p in range(PAIRS):
+    def unrotate_into(grads, side, first_j, last_j):
+        def unrotate(i, carry):
+            lanes, rows = tile_at(i)
+            for degree in range(5):
+                js = [j for j in degree_cols(degree) if first_j <= j < last_j]
+                if not js:
+                    continue
+                ks = frame_rows(degree)
+                values = [frame[rows(2 * k + side), lanes].astype(F32) for k in ks]
+                for j in js:
+                    value = None
+                    for n, k in enumerate(ks):
+                        term = factor_of(k * COEF + j, lanes) * values[n]
+                        value = term if value is None else value + term
+                    grads[rows(j), lanes] = value.astype(BF16)
+            return carry
+
+        return unrotate
+
+    def scatter(marks, grads, to, lead, first_j, last_j):
+        for p in range(first_j // 2, (last_j + 1) // 2):
             both = dot_t(marks[...], grads[2 * p * C : 2 * (p + 1) * C, :])
             for j in (2 * p, 2 * p + 1):
                 if j < COEF:
@@ -512,10 +521,29 @@
                     else:
                         to[:, :, j] = value
 
-    scatter(mark_s, xs, src_sum, (4, 2))
-    sib = net.push(src_sum.at[:, 1], reduce_scratch[2], net.sibling)
-    scatter(mark_t, xf, tgt_sum, (4, 2, 4))
-    reduce_body(net, sib, tgt_sum, src_sum, out, reduce_scratch)
+    unrotate_src = unrotate_into(xs, 0, 0, COEF)
+    unrotate_high = unrotate_into(xf, 1, *HALVES[1])
+    unrotate_low = unrotate_into(xf, 1, *HALVES[0])
+    back = Reduction(net, tgt_sum, src_sum, out, reduce_scratch)
+    lax.fori_loop(0, steps, unrotate_src, 0)
+    scatter(mark_s, xs, src_sum, (4, 2), 0, COEF)
+    back.start_rows()
+    lax.fori_loop(0, steps, unrotate_high, 0)
+    scatter(mark_t, xf, tgt_sum, (4, 2, 4), *HALVES[1])
+    back.start(1)
+    lax.fori_loop(0, steps, unrotate_low, 0)
+    back.send_rows()
+    scatter(mark_t, xf, tgt_sum, (4, 2, 4), *HALVES[0])
+    back.start(0)
+    back.join(1)
+    net.settle(back.before)
+    back.join(0)
+    final_high = back.spread(1)
+    final_low = back.spread(0)
+    back.add_rows()
+    net.settle(len(net.copies))
+    back.close(1, final_high)
+    back.close(0, final_low)
 
 
 def fused(count, src_ids, tgt_ids, rot, feats, cots, w0, w1, w2):

time: 79.9 us -> 79 us (0.989)
  no operation moved by 1% of the time
where the time goes in v7:
time: 79 us; the launch traced here: 78.9 us
  Pallas kernels  76.7 us (97%)
  local copies, waits for them, and re-layouts  1.54 us (2%)
    pallas_call x1, Pallas kernels, fused(): pl.pallas_call(fused_kernel, out_shape=jax.ShapeDtypeStruct((COEF, A, C),...  76.7 us

profile of v7, /device:TPU:2, one launch (start us, length us, event | category | flops | bytes accessed | tf_op | source)
XLA Modules:
  0.0 78.9 jit_solution(6142808332321871235)
XLA Ops:
  0.7 76.7 %edge_gradients.1 = f32[25,8,128]{2,1,0:T(8,128)} custom-call(s32[1,1]{1,0:T(1,128)S(6)} %copy.11.count, s32[1,512]{1,0:T(1,128)} %bitcast.12, s32[1,512]{1,0:T(1,128)} %bitcast.13, bf16[475,512]{1,0:T(8,128)(2,1)} %bitcast.8, bf16[25,8,128]{2,1,0:T(8,128)(2,1)} %bitcast.10, bf16[25,8,128]{2,1,0:T(8,128)(2,1)} %bitcast.11, bf16[1280,640]{1,0:T(8,128)(2,1)} %w0.1, ...), custom_call_target="tpu_custom_call" | custom-call | tf_op jit(solution)/shard_map/edge_gradients/pallas_call | solution.py:597
  77.3 1.5 %copy.12 = f32[8,25,128]{2,0,1:T(8,128)} copy(f32[8,25,128]{2,0,1:T(8,128)} %bitcast.9) | data formatting | bytes 204800

commit v8 on v7

--- a/solution.py
+++ b/solution.py
@@ -297,7 +297,7 @@
 
 def fused_kernel(
     count, src_ids, tgt_ids, rot, feats, cots, w0, w1, w2, out,
-    gf, gc, gs, w0_in, full1, full2, w0_flip, flip1, flip2, rot_wide, mark_t, mark_s,
+    g, gs, w0_in, full1, full2, w0_flip, flip1, flip2, rot_wide, mark_t, mark_s,
     xf, xc, xs, frame, grad_y, y, tgt_sum, src_sum, local_sem, send, recv, *reduce_scratch,
 ):
     net = Net(send, recv)
@@ -314,17 +314,16 @@
                     )
                 )
     mine = [
-        pltpu.make_async_copy(feats, gf.at[0, 0, 0], local_sem.at[9]),
-        pltpu.make_async_copy(cots, gc.at[0, 0, 0], local_sem.at[10]),
-        pltpu.make_async_copy(feats, gs.at[0, 0], local_sem.at[11]),
+        pltpu.make_async_copy(feats, gs.at[0, 0], local_sem.at[9]),
     ]
     for copy in mine + loads:
         copy.start()
+    g[0, 0, 0, :, :, 0:C] = feats[...]
+    g[0, 0, 0, :, :, C : 2 * C] = cots[...]
     net.greet()
 
-    first = Flow(net, feats, gf)
-    second = Flow(net, cots, gc)
-    first.send_own()
+    flow = Flow(net, g.at[0, 0, 0], g)
+    flow.send_own()
     sibling = [net.push(feats, gs.at[0, 1], net.sibling)]
     rows = [net.push(feats, gs.at[4 - step, 0], net.along_high[step]) for step in (1, 3, 2)]
     for copy in mine:
@@ -342,11 +341,10 @@
     near_core = ((ids >> 3) & 1) ^ net.core
     ids = near_high * 16 + near_core * 8 + (ids & 7)
     mark_s[...] = hot(jnp.where(valid, ids, -1), (SRC, E))
-    first.spread(0, 1)
+    flow.spread(0, 1)
     rot_wide[...] = rot[...].astype(F32)
     for inner in (3, 1, 2):
-        first.spread(inner, 2)
-    second.send_own()
+        flow.spread(inner, 2)
 
     def flip_zero(r, carry):
         at = pl.ds(pl.multiple_of(r * BLOCK, BLOCK), BLOCK)
@@ -375,14 +373,20 @@
 
         lax.fori_loop(0, k // BLOCK, body, 0)
 
-    def gather_some(marks, full, rows, to):
+    def gather_src():
         for p in range(PAIRS):
-            both = []
-            for j in (2 * p, min(2 * p + 1, COEF - 1)):
-                piece = full[:, :, :, j] if len(full.shape) == 6 else full[:, :, j]
-                both.append(piece.astype(F32).reshape(rows, C))
+            both = [
+                gs[:, :, j].astype(F32).reshape(SRC, C) for j in (2 * p, min(2 * p + 1, COEF - 1))
+            ]
             block = jnp.concatenate(both, axis=1).astype(BF16)
-            to[2 * p * C : 2 * (p + 1) * C, :] = t_dot(block, marks[...]).astype(BF16)
+            xs[2 * p * C : 2 * (p + 1) * C, :] = t_dot(block, mark_s[...]).astype(BF16)
+
+    def gather_tgt():
+        for j in range(COEF):
+            block = g[:, :, :, j].astype(F32).reshape(TGT, 2 * C).astype(BF16)
+            both = t_dot(block, mark_t[...]).astype(BF16)
+            xf[j * C : (j + 1) * C, :] = both[0:C]
+            xc[j * C : (j + 1) * C, :] = both[C : 2 * C]
 
     def factor_of(entry, lanes):
         return jnp.broadcast_to(rot_wide[entry : entry + 1, lanes], (GROUP, LANES))
@@ -427,33 +431,24 @@
     for copy in loads:
         copy.wait()
     lax.fori_loop(0, w0.shape[0] // BLOCK, flip_zero, 0)
-    first.relay(0)
+    flow.relay(0)
     for step, copy in zip((1, 3, 2), rows):
         copy.wait_recv()
         sibling.append(net.push(gs.at[4 - step, 0], gs.at[4 - step, 1], net.sibling))
-    first.relay(3)
-    first.relay(1)
-    second.spread(0, 1)
     flip_order(w2, full2, flip2)
-    first.relay(2)
-    for inner in (3, 1, 2):
-        second.spread(inner, 2)
+    flow.relay(3)
+    flow.relay(1)
     flip_order(w1, full1, flip1)
-    second.relay(0)
     for copy in sibling:
         copy.wait_recv()
-    gather_some(mark_s, gs, SRC, xs)
-    second.relay(3)
-    second.relay(1)
+    gather_src()
+    flow.relay(2)
     lax.fori_loop(0, steps, rotate_src, 0)
-    second.relay(2)
     lax.fori_loop(0, E // BLOCK, forward_src, 0)
-    first.finish()
-    gather_some(mark_t, gf, TGT, xf)
+    flow.finish()
+    gather_tgt()
     lax.fori_loop(0, steps, rotate_tgt, 0)
     lax.fori_loop(0, E // BLOCK, forward_tgt, 0)
-    second.finish()
-    gather_some(mark_t, gc, TGT, xc)
 
     def gate(i, carry):
         lanes, rows = tile_at(i)
@@ -551,8 +546,7 @@
         return pltpu.VMEM(lead + (A, C), BF16)
 
     scratch = [
-        buffer(4, 2, 4, COEF),
-        buffer(4, 2, 4, COEF),
+        pltpu.VMEM((4, 2, 4, COEF, A, 2 * C), BF16),
         buffer(4, 2, COEF),
         pltpu.VMEM(w0.shape, BF16),
         pltpu.VMEM((2 * w1.shape[1], 2 * w1.shape[2]), BF16),

time: 79 us -> 77.2 us (0.977)
  Pallas kernels: 76.7 us -> 74.8 us
    pallas_call x1, Pallas kernels: 76.7 us -> 74.8 us  [fused(): pl.pallas_call(fused_kernel, out_shape=jax.ShapeDtypeStruct((COEF, A, C),...]
where the time goes in v8:
time: 77.2 us; the launch traced here: 77.1 us
  Pallas kernels  74.8 us (97%)
  local copies, waits for them, and re-layouts  1.54 us (2%)
    pallas_call x1, Pallas kernels, fused(): pl.pallas_call(fused_kernel, out_shape=jax.ShapeDtypeStruct((COEF, A, C),...  74.8 us

profile of v8, /device:TPU:2, one launch (start us, length us, event | category | flops | bytes accessed | tf_op | source)
XLA Modules:
  0.0 77.1 jit_solution(3366539386702813105)
XLA Ops:
  0.7 74.8 %edge_gradients.1 = f32[25,8,128]{2,1,0:T(8,128)} custom-call(s32[1,1]{1,0:T(1,128)S(6)} %copy.11.count, s32[1,512]{1,0:T(1,128)} %bitcast.12, s32[1,512]{1,0:T(1,128)} %bitcast.13, bf16[475,512]{1,0:T(8,128)(2,1)} %bitcast.8, bf16[25,8,128]{2,1,0:T(8,128)(2,1)} %bitcast.10, bf16[25,8,128]{2,1,0:T(8,128)(2,1)} %bitcast.11, bf16[1280,640]{1,0:T(8,128)(2,1)} %w0.1, ...), custom_call_target="tpu_custom_call" | custom-call | tf_op jit(solution)/shard_map/edge_gradients/pallas_call | solution.py:591
  75.5 1.5 %copy.12 = f32[8,25,128]{2,0,1:T(8,128)} copy(f32[8,25,128]{2,0,1:T(8,128)} %bitcast.9) | data formatting | bytes 204800

commit v9 on v8

--- a/solution.py
+++ b/solution.py
@@ -19,6 +19,7 @@
 FRAME = 19
 GROUP = 16
 BLOCK = 256
+WIDE = 512
 LANES = 128
 TGT = COLS * A
 SRC = ROWS * A
@@ -412,7 +413,7 @@
 
     def forward_from(side):
         def forward(i, carry):
-            at = pl.ds(pl.multiple_of(i * BLOCK, BLOCK), BLOCK)
+            at = pl.ds(pl.multiple_of(i * WIDE, WIDE), WIDE)
             for begin, rows, plain, turned in parts:
                 into = slice(begin * C, (begin + rows) * C)
                 base = side * FRAME * C
@@ -444,11 +445,11 @@
     gather_src()
     flow.relay(2)
     lax.fori_loop(0, steps, rotate_src, 0)
-    lax.fori_loop(0, E // BLOCK, forward_src, 0)
+    lax.fori_loop(0, E // WIDE, forward_src, 0)
     flow.finish()
     gather_tgt()
     lax.fori_loop(0, steps, rotate_tgt, 0)
-    lax.fori_loop(0, E // BLOCK, forward_tgt, 0)
+    lax.fori_loop(0, E // WIDE, forward_tgt, 0)
 
     def gate(i, carry):
         lanes, rows = tile_at(i)
@@ -476,14 +477,14 @@
     lax.fori_loop(0, steps, gate, 0)
 
     def backward(i, carry):
-        at = pl.ds(pl.multiple_of(i * BLOCK, BLOCK), BLOCK)
+        at = pl.ds(pl.multiple_of(i * WIDE, WIDE), WIDE)
         for begin, rows, weights, turned in parts:
             frame[2 * begin * C : 2 * (begin + rows) * C, at] = dot(
                 weights[...], grad_y[begin * C : (begin + rows) * C, at]
             ).astype(BF16)
         return carry
 
-    lax.fori_loop(0, E // BLOCK, backward, 0)
+    lax.fori_loop(0, E // WIDE, backward, 0)
 
     def unrotate_into(grads, side, first_j, last_j):
         def unrotate(i, carry):

time: 77.2 us -> 76.7 us (level)
  no operation moved by 1% of the time
where the time goes in v9:
time: 76.7 us; the launch traced here: 76.5 us
  Pallas kernels  74.3 us (97%)
  local copies, waits for them, and re-layouts  1.54 us (2%)
    pallas_call x1, Pallas kernels, fused(): pl.pallas_call(fused_kernel, out_shape=jax.ShapeDtypeStruct((COEF, A, C),...  74.3 us
    unnamed x1, local copies, waits for them, and re-layouts  1.54 us

profile of v9, /device:TPU:2, one launch (start us, length us, event | category | flops | bytes accessed | tf_op | source)
XLA Modules:
  0.0 76.5 jit_solution(14746745586604651943)
XLA Ops:
  0.7 74.3 %edge_gradients.1 = f32[25,8,128]{2,1,0:T(8,128)} custom-call(s32[1,1]{1,0:T(1,128)S(6)} %copy.11.count, s32[1,512]{1,0:T(1,128)} %bitcast.12, s32[1,512]{1,0:T(1,128)} %bitcast.13, bf16[475,512]{1,0:T(8,128)(2,1)} %bitcast.8, bf16[25,8,128]{2,1,0:T(8,128)(2,1)} %bitcast.10, bf16[25,8,128]{2,1,0:T(8,128)(2,1)} %bitcast.11, bf16[1280,640]{1,0:T(8,128)(2,1)} %w0.1, ...), custom_call_target="tpu_custom_call" | custom-call | tf_op jit(solution)/shard_map/edge_gradients/pallas_call | solution.py:592
  75.0 1.5 %copy.12 = f32[8,25,128]{2,0,1:T(8,128)} copy(f32[8,25,128]{2,0,1:T(8,128)} %bitcast.9) | data formatting | bytes 204800
